TPU v7x, 128 devices: a whole 4x4x4 slice. The times are simulated.
128 devices in a mesh: tm: 16 (over x_lo, y, core), height: 8 (over z, x_hi).
Axes of the slice: x: 4 (x_hi: 2, x_lo: 2; x = x_hi * 2 + x_lo), y: 4, z: 4, core: 2. Of those that a mesh axis runs over, the one named last changes fastest.
Arguments:
- queries: bfloat16 [16, 8, 1, 384, 256], P('tm', 'height'), may hold values from -24 to 24
- key_states: bfloat16 [16, 8, 1, 384, 256], P('tm', 'height'), may hold values from -24 to 24
- value_states: bfloat16 [16, 8, 1, 384, 256], P('tm', 'height'), may hold values from -6 to 6
- out_grad: bfloat16 [16, 8, 1, 384, 256], P('tm', 'height'), may hold values from -6 to 6
- clip_start: int32 [1], replicated, may hold values from 1 to 15
Outputs:
- attended: bfloat16 [16, 8, 1, 384, 256], P('tm', 'height')
- query_grad: bfloat16 [16, 8, 1, 384, 256], P('tm', 'height')
- key_grad: bfloat16 [16, 8, 1, 384, 256], P('tm', 'height')
- value_grad: bfloat16 [16, 8, 1, 384, 256], P('tm', 'height')
All inputs are finite; a program needn't handle non-finite values.
Results may differ from a plain program's by a relative error of at most 0.0072.
Values may be sent and summed in bfloat16 or wider, within the bound.
A program may use at most 64 MiB of HBM per device.

v0:
```python
import jax
import jax.numpy as jnp
from jax import lax
from jax.sharding import PartitionSpec as P

HEADS = 2


NEGATIVE = -1e30


def padded(block, sides, width):
    for axis, dim in sides:
        count = lax.axis_size(axis)
        forward = [(i, i + 1) for i in range(count - 1)]
        backward = [(target, source) for source, target in forward]
        low = lax.ppermute(
            lax.slice_in_dim(block, block.shape[dim] - width, None, axis=dim), axis, forward
        )
        high = lax.ppermute(lax.slice_in_dim(block, 0, width, axis=dim), axis, backward)
        block = jnp.concatenate([low, block, high], axis=dim)
    return block


def tile_mask(time_index, row_index, clip_first, time_count, row_count, width_tiles):
    offsets = jnp.arange(3, dtype=jnp.int32) - 1
    key_time = time_index + offsets
    key_row = row_index + offsets
    time_valid = (
        (key_time >= 0)
        & (key_time < time_count)
        & ((key_time >= clip_first) == (time_index >= clip_first))
    )
    row_valid = (key_row >= 0) & (key_row < row_count)
    columns = jnp.arange(width_tiles, dtype=jnp.int32)
    width_valid = jnp.abs(columns[:, None] - columns[None, :]) <= 1
    combined = (
        time_valid[:, None, None, None]
        & row_valid[None, :, None, None]
        & width_valid[None, None, :, :]
    )
    return jnp.transpose(combined, (2, 0, 1, 3)).reshape(width_tiles, 9 * width_tiles)


def times_transposed(left_rows, right_rows):
    return lax.dot_general(
        left_rows, right_rows, (((1,), (1,)), ((), ())), preferred_element_type=jnp.float32
    )


def transposed_times(left_rows, right_rows):
    return lax.dot_general(
        left_rows, right_rows, (((0,), (0,)), ((), ())), preferred_element_type=jnp.float32
    )


def head_scores(left_rows, right_rows, validity, left_tiles, right_tiles):
    scores = times_transposed(left_rows, right_rows) * left_rows.shape[1] ** (-0.5)
    tile_len = left_rows.shape[0] // left_tiles
    blocked = scores.reshape(left_tiles, tile_len, right_tiles, tile_len)
    blocked = jnp.where(validity[:, None, :, None], blocked, NEGATIVE)
    return blocked.reshape(scores.shape)


def shards(queries, key_states, value_states, out_grad, clip_start):
    time_count = lax.axis_size("tm")
    row_count = lax.axis_size("height")
    time_index = lax.axis_index("tm")
    row_index = lax.axis_index("height")
    width_tiles = queries.shape[2]
    tile_len = queries.shape[3]
    channels = queries.shape[4]
    head_dim = channels // HEADS
    local_rows = width_tiles * tile_len
    scale = head_dim ** (-0.5)
    validity = tile_mask(time_index, row_index, clip_start[0], time_count, row_count, width_tiles)
    key_pad, value_pad = (
        padded(key_states, (("tm", 0), ("height", 1)), 1),
        padded(value_states, (("tm", 0), ("height", 1)), 1),
    )
    near_keys = key_pad.reshape(9 * local_rows, channels)
    near_values = value_pad.reshape(9 * local_rows, channels)
    own_queries = queries.reshape(local_rows, channels)
    own_grad = out_grad.reshape(local_rows, channels)
    score_list, total_list, output_list = ([], [], [])
    for head_number in range(HEADS):
        lower = head_number * head_dim
        upper = lower + head_dim
        scores = head_scores(
            own_queries[:, lower:upper],
            near_keys[:, lower:upper],
            validity,
            width_tiles,
            9 * width_tiles,
        )
        row_max = jnp.max(scores, axis=1, keepdims=True)
        log_total = row_max + jnp.log(jnp.sum(jnp.exp(scores - row_max), axis=1, keepdims=True))
        weights = jnp.exp(scores - log_total).astype(jnp.bfloat16)
        output_list.append(
            jnp.dot(weights, near_values[:, lower:upper], preferred_element_type=jnp.float32)
        )
        score_list.append(scores)
        total_list.append(log_total[:, 0])
    attended = jnp.concatenate(output_list, axis=1).astype(jnp.bfloat16)
    products = jnp.sum(
        (own_grad.astype(jnp.float32) * attended.astype(jnp.float32)).reshape(
            local_rows, HEADS, head_dim
        ),
        axis=2,
    )
    log_totals = jnp.stack(total_list)
    query_parts, key_parts, value_parts = ([], [], [])
    for head_number in range(HEADS):
        lower = head_number * head_dim
        upper = lower + head_dim
        grad_head = own_grad[:, lower:upper]
        probability = jnp.exp(score_list[head_number] - log_totals[head_number][:, None])
        grad_weights = times_transposed(grad_head, near_values[:, lower:upper])
        grad_scores = (
            probability * (grad_weights - products[:, head_number : head_number + 1])
        ).astype(jnp.bfloat16)
        query_parts.append(
            jnp.dot(grad_scores, near_keys[:, lower:upper], preferred_element_type=jnp.float32)
            * scale
        )
        key_parts.append(transposed_times(grad_scores, own_queries[:, lower:upper]) * scale)
        value_parts.append(transposed_times(probability.astype(jnp.bfloat16), grad_head))
    query_grad = jnp.concatenate(query_parts, axis=1).astype(jnp.bfloat16)
    packed = jnp.concatenate(key_parts + value_parts, axis=1).reshape(
        3, 3, width_tiles, tile_len, 2 * channels
    )
    edges = jnp.stack([packed[0], packed[2]])
    arrived = padded(edges, (("tm", 0),), 1)
    middle = packed[1] + arrived[0] + arrived[3]
    edges = jnp.stack([middle[0], middle[2]])
    arrived = padded(edges, (("height", 0),), 1)
    combined = middle[1] + arrived[0] + arrived[3]
    key_grad = combined[..., :channels].astype(jnp.bfloat16).reshape(key_states.shape)
    value_grad = combined[..., channels:].astype(jnp.bfloat16).reshape(value_states.shape)
    return (
        attended.reshape(queries.shape),
        query_grad.reshape(queries.shape),
        key_grad,
        value_grad,
    )


def solution(mesh):
    return jax.shard_map(
        shards,
        mesh=mesh,
        in_specs=(
            P("tm", "height", None, None, None),
            P("tm", "height", None, None, None),
            P("tm", "height", None, None, None),
            P("tm", "height", None, None, None),
            P(),
        ),
        out_specs=(
            P("tm", "height", None, None, None),
            P("tm", "height", None, None, None),
            P("tm", "height", None, None, None),
            P("tm", "height", None, None, None),
        ),
        check_vma=False,
    )
```

profile of v0, /device:TPU:6, one launch (start us, length us, event | category | flops | bytes accessed | tf_op | source)
XLA Modules:
  0.0 171.7 jit_solution(3570368387454265992)
XLA Ops:
  0.6 1.9 %collective-permute-start = (bf16[1,1,1,384,256]{4,3,2,1,0:T(8,128)(2,1)}, bf16[1,1,1,384,256]{4,3,2,1,0:T(8,128)(2,1)S(1)}, u32[]{:S(2)}, u32[]{:S(2)}) collective-permute-start(bf16[1,1,1,384,256]{4,3,2,1,0:T(8,128)(2,1)} %param.6), channel_id=1, source_target_pairs={{0,8},{8,16},{16,24},{24,32},{32,40},{40,48},{48,56},{56,64},{64,7... | collective-permute-start | bytes 589832 | tf_op jit(solution)/shard_map/ppermute | solution.py:17
  2.6 5.8 %collective-permute-start.1 = (bf16[1,1,1,384,256]{4,3,2,1,0:T(8,128)(2,1)}, bf16[1,1,1,384,256]{4,3,2,1,0:T(8,128)(2,1)S(1)}, u32[]{:S(2)}, u32[]{:S(2)}) collective-permute-start(bf16[1,1,1,384,256]{4,3,2,1,0:T(8,128)(2,1)} %param.6), channel_id=1, source_target_pairs={{8,0},{16,8},{24,16},{32,24},{40,32},{48,40},{56,48},{64,56},{72,6... | collective-permute-start | bytes 589832 | tf_op jit(solution)/shard_map/ppermute | solution.py:20
  8.3 1.6 collective-permute-done
  11.8 3.3 %collective-permute-start.3 = (bf16[3,1,1,384,256]{4,3,2,1,0:T(8,128)(2,1)S(1)}, bf16[3,1,1,384,256]{4,3,2,1,0:T(8,128)(2,1)S(1)}, u32[]{:S(2)}, u32[]{:S(2)}) collective-permute-start(bf16[3,1,1,384,256]{4,3,2,1,0:T(8,128)(2,1)S(1)} %constant_dynamic-update-slice_fusion), channel_id=1, source_target_pairs={{1,0},{2,1},{3,2},{4,3},{5,4},{6,5},{7,6},{9,8},{10,9},{11,10},{12... | collective-permute-start | bytes 1769480 | tf_op jit(solution)/shard_map/ppermute | solution.py:20
  15.1 4.9 %collective-permute-start.2 = (bf16[3,1,1,384,256]{4,3,2,1,0:T(8,128)(2,1)S(1)}, bf16[3,1,1,384,256]{4,3,2,1,0:T(8,128)(2,1)S(1)}, u32[]{:S(2)}, u32[]{:S(2)}) collective-permute-start(bf16[3,1,1,384,256]{4,3,2,1,0:T(8,128)(2,1)S(1)} %constant_dynamic-update-slice_fusion), channel_id=1, source_target_pairs={{0,1},{1,2},{2,3},{3,4},{4,5},{5,6},{6,7},{8,9},{9,10},{10,11},{11... | collective-permute-start | bytes 1769480 | tf_op jit(solution)/shard_map/ppermute | solution.py:17
  20.1 1.9 %collective-permute-start.4 = (bf16[1,1,1,384,256]{4,3,2,1,0:T(8,128)(2,1)}, bf16[1,1,1,384,256]{4,3,2,1,0:T(8,128)(2,1)S(1)}, u32[]{:S(2)}, u32[]{:S(2)}) collective-permute-start(bf16[1,1,1,384,256]{4,3,2,1,0:T(8,128)(2,1)} %param.7), channel_id=1, source_target_pairs={{0,8},{8,16},{16,24},{24,32},{32,40},{40,48},{48,56},{56,64},{64,7... | collective-permute-start | bytes 589832 | tf_op jit(solution)/shard_map/ppermute | solution.py:17
  22.0 5.8 %collective-permute-start.5 = (bf16[1,1,1,384,256]{4,3,2,1,0:T(8,128)(2,1)}, bf16[1,1,1,384,256]{4,3,2,1,0:T(8,128)(2,1)S(1)}, u32[]{:S(2)}, u32[]{:S(2)}) collective-permute-start(bf16[1,1,1,384,256]{4,3,2,1,0:T(8,128)(2,1)} %param.7), channel_id=1, source_target_pairs={{8,0},{16,8},{24,16},{32,24},{40,32},{48,40},{56,48},{64,56},{72,6... | collective-permute-start | bytes 589832 | tf_op jit(solution)/shard_map/ppermute | solution.py:20
  29.9 19.0 %collective-permute-done.4 = bf16[1,1,1,384,256]{4,3,2,1,0:T(8,128)(2,1)S(1)} collective-permute-done((bf16[1,1,1,384,256]{4,3,2,1,0:T(8,128)(2,1)}, bf16[1,1,1,384,256]{4,3,2,1,0:T(8,128)(2,1)S(1)}, u32[]{:S(2)}, u32[]{:S(2)}) %collective-permute-start.4) | collective-permute-done | bytes 196640 | tf_op jit(solution)/shard_map/ppermute | solution.py:17
  49.9 1.9 %collective-permute-start.7 = (bf16[3,1,1,384,256]{4,3,2,1,0:T(8,128)(2,1)S(1)}, bf16[3,1,1,384,256]{4,3,2,1,0:T(8,128)(2,1)S(1)}, u32[]{:S(2)}, u32[]{:S(2)}) collective-permute-start(bf16[3,1,1,384,256]{4,3,2,1,0:T(8,128)(2,1)S(1)} %constant_dynamic-update-slice_fusion.3), channel_id=1, source_target_pairs={{1,0},{2,1},{3,2},{4,3},{5,4},{6,5},{7,6},{9,8},{10,9},{11,10},{12... | collective-permute-start | bytes 1769480 | tf_op jit(solution)/shard_map/ppermute | solution.py:20
  51.9 6.3 %collective-permute-start.6 = (bf16[3,1,1,384,256]{4,3,2,1,0:T(8,128)(2,1)S(1)}, bf16[3,1,1,384,256]{4,3,2,1,0:T(8,128)(2,1)S(1)}, u32[]{:S(2)}, u32[]{:S(2)}) collective-permute-start(bf16[3,1,1,384,256]{4,3,2,1,0:T(8,128)(2,1)S(1)} %constant_dynamic-update-slice_fusion.3), channel_id=1, source_target_pairs={{0,1},{1,2},{2,3},{3,4},{4,5},{5,6},{6,7},{8,9},{9,10},{10,11},{11... | collective-permute-start | bytes 1769480 | tf_op jit(solution)/shard_map/ppermute | solution.py:17
  58.4 1.2 fusion.39
  60.6 1.2 fusion.40
  61.8 2.9 %collective-permute-done.7 = bf16[3,1,1,384,256]{4,3,2,1,0:T(8,128)(2,1)S(1)} collective-permute-done((bf16[3,1,1,384,256]{4,3,2,1,0:T(8,128)(2,1)S(1)}, bf16[3,1,1,384,256]{4,3,2,1,0:T(8,128)(2,1)S(1)}, u32[]{:S(2)}, u32[]{:S(2)}) %collective-permute-start.7) | collective-permute-done | bytes 589856 | tf_op jit(solution)/shard_map/ppermute | solution.py:20
  64.7 2.8 %collective-permute-done.6 = bf16[3,1,1,384,256]{4,3,2,1,0:T(8,128)(2,1)S(1)} collective-permute-done((bf16[3,1,1,384,256]{4,3,2,1,0:T(8,128)(2,1)S(1)}, bf16[3,1,1,384,256]{4,3,2,1,0:T(8,128)(2,1)S(1)}, u32[]{:S(2)}, u32[]{:S(2)}) %collective-permute-start.6) | collective-permute-done | bytes 589856 | tf_op jit(solution)/shard_map/ppermute | solution.py:17
  75.9 1.5 copy-done
  79.2 3.1 %fusion.37 = (f32[1152,512]{0,1:T(8,128)}, f32[1152,512]{0,1:T(8,128)}, f32[1152,512]{0,1:T(8,128)}) fusion(f32[3456,512]{0,1:T(8,128)S(1)} %pad_maximum_fusion), kind=kLoop, calls=%fused_computation.71 | loop fusion | bytes 14155776 | tf_op jit(solution)/shard_map/slice | solution.py:132
  82.3 3.1 %copy.17 = f32[1152,512]{1,0:T(8,128)} copy(f32[1152,512]{0,1:T(8,128)} %get-tuple-element.14) | data formatting | bytes 4718592 | tf_op jit(solution)/shard_map/slice | solution.py:132
  85.4 3.2 %copy.18 = f32[1152,512]{1,0:T(8,128)} copy(f32[1152,512]{0,1:T(8,128)} %get-tuple-element.15) | data formatting | bytes 4718592 | tf_op jit(solution)/shard_map/slice | solution.py:132
  88.5 3.2 %collective-permute-start.9 = (f32[1,3,1,384,512]{4,3,1,2,0:T(8,128)}, f32[1,3,1,384,512]{4,3,1,2,0:T(8,128)}, u32[]{:S(2)}, u32[]{:S(2)}) collective-permute-start(f32[1,3,1,384,512]{4,3,1,2,0:T(8,128)} %bitcast.47), channel_id=1, source_target_pairs={{8,0},{16,8},{24,16},{32,24},{40,32},{48,40},{56,48},{64,56},{72,6... | collective-permute-start | bytes 7077896 | tf_op jit(solution)/shard_map/ppermute | solution.py:20
  91.7 1.9 %collective-permute-start.8 = (f32[1,3,1,384,512]{4,3,1,2,0:T(8,128)}, f32[1,3,1,384,512]{4,3,1,2,0:T(8,128)}, u32[]{:S(2)}, u32[]{:S(2)}) collective-permute-start(f32[1,3,1,384,512]{4,3,1,2,0:T(8,128)} %bitcast.46), channel_id=1, source_target_pairs={{0,8},{8,16},{16,24},{24,32},{32,40},{40,48},{48,56},{56,64},{64,7... | collective-permute-start | bytes 7077896 | tf_op jit(solution)/shard_map/ppermute | solution.py:17
  93.7 3.1 %copy.16 = f32[1152,512]{1,0:T(8,128)} copy(f32[1152,512]{0,1:T(8,128)} %get-tuple-element.16) | data formatting | bytes 4718592 | tf_op jit(solution)/shard_map/slice | solution.py:134
  96.8 21.6 %collective-permute-done.9 = f32[1,3,1,384,512]{4,3,1,2,0:T(8,128)} collective-permute-done((f32[1,3,1,384,512]{4,3,1,2,0:T(8,128)}, f32[1,3,1,384,512]{4,3,1,2,0:T(8,128)}, u32[]{:S(2)}, u32[]{:S(2)}) %collective-permute-start.9) | collective-permute-done | bytes 2359328 | tf_op jit(solution)/shard_map/ppermute | solution.py:20
  118.4 5.9 %collective-permute-done.8 = f32[1,3,1,384,512]{4,3,1,2,0:T(8,128)} collective-permute-done((f32[1,3,1,384,512]{4,3,1,2,0:T(8,128)}, f32[1,3,1,384,512]{4,3,1,2,0:T(8,128)}, u32[]{:S(2)}, u32[]{:S(2)}) %collective-permute-start.8) | collective-permute-done | bytes 2359328 | tf_op jit(solution)/shard_map/ppermute | solution.py:17
  124.3 3.9 %bitcast_add_fusion = f32[3,1,384,512]{3,2,0,1:T(8,128)S(1)} fusion(f32[1,3,1,384,512]{4,3,1,2,0:T(8,128)} %collective-permute-done.9, f32[3,1,384,512]{3,2,0,1:T(8,128)} %bitcast.41, f32[1,3,1,384,512]{4,3,1,2,0:T(8,128)} %collective-permute-done.8), kind=kLoop, calls=%fused_computation.19 | loop fusion | flops 1179648 | bytes 9437184 | tf_op jit(solution)/shard_map/add | solution.py:134
  128.3 1.4 copy-done.2
  129.7 1.3 fusion.38
  131.0 7.1 %collective-permute-start.10 = (f32[1,1,384,512]{3,2,0,1:T(8,128)}, f32[1,1,384,512]{3,2,0,1:T(8,128)}, u32[]{:S(2)}, u32[]{:S(2)}) collective-permute-start(f32[1,1,384,512]{3,2,0,1:T(8,128)} %get-tuple-element.17), channel_id=1, source_target_pairs={{0,1},{1,2},{2,3},{3,4},{4,5},{5,6},{6,7},{8,9},{9,10},{10,11},{11... | collective-permute-start | bytes 2359304 | tf_op jit(solution)/shard_map/ppermute | solution.py:17
  138.1 1.9 %collective-permute-start.11 = (f32[1,1,384,512]{3,2,0,1:T(8,128)}, f32[1,1,384,512]{3,2,0,1:T(8,128)}, u32[]{:S(2)}, u32[]{:S(2)}) collective-permute-start(f32[1,1,384,512]{3,2,0,1:T(8,128)} %get-tuple-element.18), channel_id=1, source_target_pairs={{1,0},{2,1},{3,2},{4,3},{5,4},{6,5},{7,6},{9,8},{10,9},{11,10},{12... | collective-permute-start | bytes 2359304 | tf_op jit(solution)/shard_map/ppermute | solution.py:20
  140.9 2.0 %fusion.10 = bf16[1,1,1,384,128]{3,4,2,1,0:T(8,128)(2,1)S(1)} fusion(bf16[3456,384]{1,0:T(8,128)(2,1)S(1)} %fusion.5, bf16[3456,256]{1,0:T(8,128)(2,1)} %bitcast.44), kind=kOutput, calls=%fused_computation.29 | convolution fusion | flops 339836928 | bytes 3637248 | tf_op jit(solution)/shard_map/dot_general | solution.py:123
  145.0 11.4 %collective-permute-done.10 = f32[1,1,384,512]{3,2,0,1:T(8,128)} collective-permute-done((f32[1,1,384,512]{3,2,0,1:T(8,128)}, f32[1,1,384,512]{3,2,0,1:T(8,128)}, u32[]{:S(2)}, u32[]{:S(2)}) %collective-permute-start.10) | collective-permute-done | bytes 786464 | tf_op jit(solution)/shard_map/ppermute | solution.py:17
  156.4 12.7 %collective-permute-done.11 = f32[1,1,384,512]{3,2,0,1:T(8,128)} collective-permute-done((f32[1,1,384,512]{3,2,0,1:T(8,128)}, f32[1,1,384,512]{3,2,0,1:T(8,128)}, u32[]{:S(2)}, u32[]{:S(2)}) %collective-permute-start.11) | collective-permute-done | bytes 786464 | tf_op jit(solution)/shard_map/ppermute | solution.py:20
  169.1 1.8 %fusion.28 = bf16[1,384,512]{2,1,0:T(8,128)(2,1)S(1)} fusion(f32[1,1,384,512]{3,2,0,1:T(8,128)} %collective-permute-done.11, f32[1,1,384,512]{3,2,0,1:T(8,128)} %collective-permute-done.10, f32[3,1,384,512]{3,2,0,1:T(8,128)} %copy-done.2), kind=kLoop, calls=%fused_computation.44 | loop fusion | flops 589824 | bytes 2752512 | tf_op jit(solution)/shard_map/convert.2
  (55 shorter events, 19.1 us)
Async XLA Ops:
  0.6 9.3 %collective-permute-start = (bf16[1,1,1,384,256]{4,3,2,1,0:T(8,128)(2,1)}, bf16[1,1,1,384,256]{4,3,2,1,0:T(8,128)(2,1)S(1)}, u32[]{:S(2)}, u32[]{:S(2)}) collective-permute-start(bf16[1,1,1,384,256]{4,3,2,1,0:T(8,128)(2,1)} %param.6), channel_id=1, source_target_pairs={{0,8},{8,16},{16,24},{24,32},{32,40},{40,48},{48,56},{56,64},{64,7... | collective-permute-start | bytes 589832 | tf_op jit(solution)/shard_map/ppermute | solution.py:17
  2.6 9.2 %collective-permute-start.1 = (bf16[1,1,1,384,256]{4,3,2,1,0:T(8,128)(2,1)}, bf16[1,1,1,384,256]{4,3,2,1,0:T(8,128)(2,1)S(1)}, u32[]{:S(2)}, u32[]{:S(2)}) collective-permute-start(bf16[1,1,1,384,256]{4,3,2,1,0:T(8,128)(2,1)} %param.6), channel_id=1, source_target_pairs={{8,0},{16,8},{24,16},{32,24},{40,32},{48,40},{56,48},{64,56},{72,6... | collective-permute-start | bytes 589832 | tf_op jit(solution)/shard_map/ppermute | solution.py:20
  11.8 46.4 %collective-permute-start.3 = (bf16[3,1,1,384,256]{4,3,2,1,0:T(8,128)(2,1)S(1)}, bf16[3,1,1,384,256]{4,3,2,1,0:T(8,128)(2,1)S(1)}, u32[]{:S(2)}, u32[]{:S(2)}) collective-permute-start(bf16[3,1,1,384,256]{4,3,2,1,0:T(8,128)(2,1)S(1)} %constant_dynamic-update-slice_fusion), channel_id=1, source_target_pairs={{1,0},{2,1},{3,2},{4,3},{5,4},{6,5},{7,6},{9,8},{10,9},{11,10},{12... | collective-permute-start | bytes 1769480 | tf_op jit(solution)/shard_map/ppermute | solution.py:20
  15.1 43.1 %collective-permute-start.2 = (bf16[3,1,1,384,256]{4,3,2,1,0:T(8,128)(2,1)S(1)}, bf16[3,1,1,384,256]{4,3,2,1,0:T(8,128)(2,1)S(1)}, u32[]{:S(2)}, u32[]{:S(2)}) collective-permute-start(bf16[3,1,1,384,256]{4,3,2,1,0:T(8,128)(2,1)S(1)} %constant_dynamic-update-slice_fusion), channel_id=1, source_target_pairs={{0,1},{1,2},{2,3},{3,4},{4,5},{5,6},{6,7},{8,9},{9,10},{10,11},{11... | collective-permute-start | bytes 1769480 | tf_op jit(solution)/shard_map/ppermute | solution.py:17
  20.1 28.9 %collective-permute-start.4 = (bf16[1,1,1,384,256]{4,3,2,1,0:T(8,128)(2,1)}, bf16[1,1,1,384,256]{4,3,2,1,0:T(8,128)(2,1)S(1)}, u32[]{:S(2)}, u32[]{:S(2)}) collective-permute-start(bf16[1,1,1,384,256]{4,3,2,1,0:T(8,128)(2,1)} %param.7), channel_id=1, source_target_pairs={{0,8},{8,16},{16,24},{24,32},{32,40},{40,48},{48,56},{56,64},{64,7... | collective-permute-start | bytes 589832 | tf_op jit(solution)/shard_map/ppermute | solution.py:17
  22.0 27.9 %collective-permute-start.5 = (bf16[1,1,1,384,256]{4,3,2,1,0:T(8,128)(2,1)}, bf16[1,1,1,384,256]{4,3,2,1,0:T(8,128)(2,1)S(1)}, u32[]{:S(2)}, u32[]{:S(2)}) collective-permute-start(bf16[1,1,1,384,256]{4,3,2,1,0:T(8,128)(2,1)} %param.7), channel_id=1, source_target_pairs={{8,0},{16,8},{24,16},{32,24},{40,32},{48,40},{56,48},{64,56},{72,6... | collective-permute-start | bytes 589832 | tf_op jit(solution)/shard_map/ppermute | solution.py:20
  28.8 29.6 %copy-start.6 = (bf16[1,1,1,384,256]{4,3,2,1,0:T(8,128)(2,1)S(1)}, bf16[1,1,1,384,256]{4,3,2,1,0:T(8,128)(2,1)}, u32[]{:S(2)}) copy-start(bf16[1,1,1,384,256]{4,3,2,1,0:T(8,128)(2,1)} %param.5) | copy-start | bytes 589828
  49.9 14.8 %collective-permute-start.7 = (bf16[3,1,1,384,256]{4,3,2,1,0:T(8,128)(2,1)S(1)}, bf16[3,1,1,384,256]{4,3,2,1,0:T(8,128)(2,1)S(1)}, u32[]{:S(2)}, u32[]{:S(2)}) collective-permute-start(bf16[3,1,1,384,256]{4,3,2,1,0:T(8,128)(2,1)S(1)} %constant_dynamic-update-slice_fusion.3), channel_id=1, source_target_pairs={{1,0},{2,1},{3,2},{4,3},{5,4},{6,5},{7,6},{9,8},{10,9},{11,10},{12... | collective-permute-start | bytes 1769480 | tf_op jit(solution)/shard_map/ppermute | solution.py:20
  51.9 15.7 %collective-permute-start.6 = (bf16[3,1,1,384,256]{4,3,2,1,0:T(8,128)(2,1)S(1)}, bf16[3,1,1,384,256]{4,3,2,1,0:T(8,128)(2,1)S(1)}, u32[]{:S(2)}, u32[]{:S(2)}) collective-permute-start(bf16[3,1,1,384,256]{4,3,2,1,0:T(8,128)(2,1)S(1)} %constant_dynamic-update-slice_fusion.3), channel_id=1, source_target_pairs={{0,1},{1,2},{2,3},{3,4},{4,5},{5,6},{6,7},{8,9},{9,10},{10,11},{11... | collective-permute-start | bytes 1769480 | tf_op jit(solution)/shard_map/ppermute | solution.py:17
  58.4 2.1 %copy-start.3 = (bf16[3,3,1,384,256]{4,3,2,1,0:T(8,128)(2,1)}, bf16[3,3,1,384,256]{4,3,2,1,0:T(8,128)(2,1)S(1)}, u32[]{:S(2)}) copy-start(bf16[3,3,1,384,256]{4,3,2,1,0:T(8,128)(2,1)S(1)} %pad_maximum_fusion.1) | copy-start | bytes 5308420
  67.7 1.0 copy-start.5
  75.9 1.5 copy-start
  88.5 29.9 %collective-permute-start.9 = (f32[1,3,1,384,512]{4,3,1,2,0:T(8,128)}, f32[1,3,1,384,512]{4,3,1,2,0:T(8,128)}, u32[]{:S(2)}, u32[]{:S(2)}) collective-permute-start(f32[1,3,1,384,512]{4,3,1,2,0:T(8,128)} %bitcast.47), channel_id=1, source_target_pairs={{8,0},{16,8},{24,16},{32,24},{40,32},{48,40},{56,48},{64,56},{72,6... | collective-permute-start | bytes 7077896 | tf_op jit(solution)/shard_map/ppermute | solution.py:20
  91.7 32.6 %collective-permute-start.8 = (f32[1,3,1,384,512]{4,3,1,2,0:T(8,128)}, f32[1,3,1,384,512]{4,3,1,2,0:T(8,128)}, u32[]{:S(2)}, u32[]{:S(2)}) collective-permute-start(f32[1,3,1,384,512]{4,3,1,2,0:T(8,128)} %bitcast.46), channel_id=1, source_target_pairs={{0,8},{8,16},{16,24},{24,32},{32,40},{40,48},{48,56},{56,64},{64,7... | collective-permute-start | bytes 7077896 | tf_op jit(solution)/shard_map/ppermute | solution.py:17
  128.3 1.4 copy-start.2
  131.0 25.4 %collective-permute-start.10 = (f32[1,1,384,512]{3,2,0,1:T(8,128)}, f32[1,1,384,512]{3,2,0,1:T(8,128)}, u32[]{:S(2)}, u32[]{:S(2)}) collective-permute-start(f32[1,1,384,512]{3,2,0,1:T(8,128)} %get-tuple-element.17), channel_id=1, source_target_pairs={{0,1},{1,2},{2,3},{3,4},{4,5},{5,6},{6,7},{8,9},{9,10},{10,11},{11... | collective-permute-start | bytes 2359304 | tf_op jit(solution)/shard_map/ppermute | solution.py:17
  138.1 31.0 %collective-permute-start.11 = (f32[1,1,384,512]{3,2,0,1:T(8,128)}, f32[1,1,384,512]{3,2,0,1:T(8,128)}, u32[]{:S(2)}, u32[]{:S(2)}) collective-permute-start(f32[1,1,384,512]{3,2,0,1:T(8,128)} %get-tuple-element.18), channel_id=1, source_target_pairs={{1,0},{2,1},{3,2},{4,3},{5,4},{6,5},{7,6},{9,8},{10,9},{11,10},{12... | collective-permute-start | bytes 2359304 | tf_op jit(solution)/shard_map/ppermute | solution.py:20
  140.9 2.0 %copy-start.1 = (bf16[3456,384]{1,0:T(8,128)(2,1)S(1)}, bf16[3456,384]{1,0:T(8,128)(2,1)}, u32[]{:S(2)}) copy-start(bf16[3456,384]{1,0:T(8,128)(2,1)} %copy-done) | copy-start | bytes 7962628
  140.9 2.5 %copy-start.4 = (bf16[3,3,1,384,256]{4,3,2,1,0:T(8,128)(2,1)S(1)}, bf16[3,3,1,384,256]{4,3,2,1,0:T(8,128)(2,1)}, u32[]{:S(2)}) copy-start(bf16[3,3,1,384,256]{4,3,2,1,0:T(8,128)(2,1)} %copy-done.3) | copy-start | bytes 5308420
where the time goes:
time: 173 us; the launch traced here: 172 us
  waiting for transfers between devices  78.9 us (46%)
  starting transfers between devices  46 us (27%)
  local copies, waits for them, and re-layouts  23 us (13%)
  matrix products  13.2 us (8%)
  other arithmetic  8.82 us (5%)
    ppermute x6, waiting for transfers between devices, padded(): lax.ppermute(lax.slice_in_dim(block, block.shape[dim] - width, None, axis...  40.8 us
    ppermute x6, waiting for transfers between devices, padded(): lax.ppermute(lax.slice_in_dim(block, 0, width, axis=dim), axis, backward)  38.1 us
    ppermute x6, starting transfers between devices, padded(): lax.ppermute(lax.slice_in_dim(block, block.shape[dim] - width, None, axis...  24.1 us
    ppermute x6, starting transfers between devices, padded(): lax.ppermute(lax.slice_in_dim(block, 0, width, axis=dim), axis, backward)  21.9 us
    slice x3, local copies, waits for them, and re-layouts, shards(): edges = jnp.stack([packed[0], packed[2]])  9.31 us
    unnamed x20, local copies, waits for them, and re-layouts  7.05 us
    dot_general x4, matrix products, times_transposed(): lax.dot_general(left_rows, right_rows, (((1,), (1,)), ((), ())), preferre...  4.73 us
    add x1, other arithmetic, shards(): middle = packed[1] + arrived[0] + arrived[3]  3.95 us
  transfers between devices with their start and end apart: 12, of which 9 were waited for; matrix products, arithmetic and copies ran while one was open for 8% of the time, Pallas kernels for 0%

commit v1 on v0

v1 whole, which is shorter than its diff:
```python
import functools

import jax
import jax.numpy as jnp
from jax import lax
from jax.experimental import pallas as pl
from jax.experimental.pallas import tpu as pltpu
from jax.sharding import PartitionSpec as P

HEADS = 2
LOG2E = 1.4426950408889634
NEGATIVE = -1e30
MESH = pl.DeviceIdType.MESH
K, V, Q, G, STATS = range(5)


def nt(left, right):
    return lax.dot_general(left, right, (((1,), (1,)), ((), ())), preferred_element_type=jnp.float32)


def nn(left, right):
    return jnp.dot(left, right, preferred_element_type=jnp.float32)


def kernel(
    clip_ref, q_in, k_in, v_in, g_in, att_out, dq_out, dk_out, dv_out,
    tiles, stats, acc, grad, row_max, row_sum, row_dot, key_acc, value_acc,
    local_sem, swap_send, swap_recv, z_send, z_recv, tm_send, tm_recv,
):
    t = lax.axis_index("tm")
    h = lax.axis_index("height")
    core, odd, z = t % 2, h % 2, h // 2
    dim = q_in.shape[-1] // HEADS
    scale = dim ** (-0.5)
    to_log2 = scale * LOG2E

    copies = [pltpu.make_async_copy(ref, tiles.at[1, 0, u], local_sem.at[u]) for u, ref in enumerate((k_in, v_in, q_in, g_in))]
    for copy in copies:
        copy.start()

    first, last = t == 0, t == 15
    left, right = t == 7, t == 8
    relay = first | last
    two = relay | left | right
    swap_dev = (t, h + 1 - 2 * odd)
    chip_dev = (t + 1 - 2 * core, h)
    z_to = jnp.where(odd == 0, z < 3, z > 0)
    z_from = jnp.where(odd == 0, z > 0, z < 3)
    z_dst = (t, h + 2 - 4 * odd)
    z_src = (t, h - 2 + 4 * odd)
    chip_there = jnp.where(core == 0, 0, 2)
    chip_here = 2 - chip_there
    off_here = chip_there
    near = jnp.where(core == 1, t + 1, t - 1)
    near_slot = jnp.where(core == 1, 0, 2)
    off_dev = (
        jnp.where(left, 15, jnp.where(right, 0, jnp.where(last, 8, jnp.where(first, 7, near)))),
        jnp.where(left, 0, jnp.where(right, 15, jnp.where(last, 7, jnp.where(first, 8, near)))),
    )
    off_slot = (
        jnp.where(left | first, 2, jnp.where(right | last, 0, near_slot)),
        jnp.where(left | first, 0, jnp.where(right | last, 2, near_slot)),
    )
    off_from = jnp.where(last, 2, jnp.where(first, 0, 1))

    barrier = pltpu.get_barrier_semaphore()

    def greet(device):
        pl.semaphore_signal(barrier, inc=1, device_id=device, device_id_type=MESH)

    greet(swap_dev)
    greet(chip_dev)
    greet((off_dev[0], h))

    @pl.when(two)
    def _():
        greet((off_dev[1], h))

    @pl.when(z_from)
    def _():
        greet(z_src)

    pl.semaphore_wait(barrier, 3 + two.astype(jnp.int32) + z_to.astype(jnp.int32))

    def part(a, s, u):
        return stats.at[a, s] if u == STATS else tiles.at[a, s, u]

    def remote(src, dst, send, recv, device):
        return pltpu.make_async_remote_copy(
            src_ref=src, dst_ref=dst, send_sem=send, recv_sem=recv, device_id=device, device_id_type=MESH
        )

    def swap(u):
        return remote(part(1, 0, u), part(1, 1, u), swap_send.at[u], swap_recv.at[u], swap_dev)

    def along_z(u):
        return remote(part(1, 1, u), part(1, 2, u), z_send.at[u], z_recv.at[u], z_dst)

    def to_chip(s, u):
        return remote(part(1, s, u), part(chip_there, s, u), tm_send.at[0, s, u], tm_recv.at[chip_there, s, u], chip_dev)

    def off_chip(s, u):
        device, slot = off_dev[u % 2], off_slot[u % 2]
        return remote(part(off_from, s, u), part(slot, s, u), tm_send.at[1, s, u], tm_recv.at[slot, s, u], (device, h))

    def arrive(a, s, u):
        remote(part(1, s, u), part(a, s, u), tm_send.at[0, s, u], tm_recv.at[a, s, u], chip_dev).wait_recv()

    def spread(s, u):
        to_chip(s, u).start()

        @pl.when(~relay)
        def _():
            off_chip(s, u).start()

    def on_swap(u):
        swap(u).wait_recv()

        @pl.when(z_to)
        def _():
            along_z(u).start()

        spread(1, u)

    def on_z(u):
        @pl.when(z_from)
        def _():
            along_z(u).wait_recv()
            spread(2, u)

    def on_relay(s, u):
        @pl.when(relay & z_from if s == 2 else relay)
        def _():
            arrive(off_here, s, u)
            off_chip(s, u).start()

    for copy in copies:
        copy.wait()
    for u in (K, V, Q, G):
        swap(u).start()
        spread(0, u)

    clip = clip_ref[0]

    def place(i):
        s, o = i // 3, i % 3
        a = jnp.where(o == 0, 1, jnp.where(o == 1, chip_here, off_here))
        there = ((s < 2) | z_from) & ((o < 2) | ~relay)
        related = ((t + a - 1) >= clip) == (t >= clip)
        return s, o, a, there, related

    def columns(n):
        return slice(n * dim, (n + 1) * dim)

    row_max[...] = jnp.full(row_max.shape, NEGATIVE, jnp.float32)
    for ref in (acc, grad, row_sum, row_dot, key_acc, value_acc):
        ref[...] = jnp.zeros(ref.shape, ref.dtype)

    first_events = {
        1: [(on_relay, 0, K)],
        2: [(on_swap, K), (on_relay, 0, V)],
        3: [(on_swap, V), (on_relay, 0, Q)],
        4: [(on_relay, 1, K), (on_z, K), (on_relay, 0, G)],
        5: [(on_swap, Q), (on_relay, 1, V)],
        6: [(on_z, V), (on_relay, 2, K)],
        7: [(on_swap, G), (on_relay, 1, Q)],
        8: [(on_z, Q), (on_relay, 2, V), (on_relay, 1, G)],
    }
    second_events = {
        1: [(on_swap, STATS), (on_relay, 0, STATS)],
        2: [(on_z, G), (on_relay, 2, Q)],
        3: [(on_z, STATS), (on_relay, 1, STATS)],
        4: [(on_relay, 2, G), (on_relay, 2, STATS)],
    }

    def run(events, i):
        for step, entries in events.items():
            @pl.when(i == step)
            def _():
                for entry in entries:
                    entry[0](*entry[1:])

    def queries_side(i, carry):
        run(first_events, i)
        s, o, a, there, related = place(i)

        @pl.when(there & (o > 0))
        def _():
            arrive(a, s, K)
            arrive(a, s, V)

        @pl.when(there)
        def _():
            for n in range(HEADS):
                own_q, own_g = tiles[1, 0, Q, :, columns(n)], tiles[1, 0, G, :, columns(n)]
                key, value = tiles[a, s, K, :, columns(n)], tiles[a, s, V, :, columns(n)]
                scores = nt(own_q, key)
                top = jnp.where(related, jnp.max(scores, axis=1, keepdims=True) * to_log2, NEGATIVE)
                old_max = row_max[n]
                new_max = jnp.maximum(old_max, top)
                fade = jnp.exp2(old_max - new_max)
                raised = jnp.exp2(scores * to_log2 - jnp.where(related, new_max, -NEGATIVE))
                total = row_sum[n] * fade + jnp.sum(raised, axis=1, keepdims=True)
                old = acc[n]
                new = old * fade + nn(raised.astype(jnp.bfloat16), jnp.concatenate([value, key], axis=1))
                old_dot = row_dot[n]
                dot = jnp.sum(own_g.astype(jnp.float32) * new[:, :dim], axis=1, keepdims=True) / total
                inner = (raised * (nt(own_g, value) - dot)).astype(jnp.bfloat16)
                grad[n] = (grad[n] - (dot - old_dot) * old[:, dim:]) * fade + nn(inner, key)
                acc[n] = new
                row_max[n] = new_max
                row_sum[n] = total
                row_dot[n] = dot

        return carry

    lax.fori_loop(0, 9, queries_side, 0)

    lanes = lax.broadcasted_iota(jnp.int32, (q_in.shape[0], 128), 1)
    table = jnp.zeros((q_in.shape[0], 128), jnp.float32)
    finish = []
    for n in range(HEADS):
        total = row_sum[n]
        sums = acc[n]
        attended = (sums[:, :dim] / total).astype(jnp.bfloat16)
        att_out[:, columns(n)] = attended
        dot = jnp.sum(tiles[1, 0, G, :, columns(n)].astype(jnp.float32) * attended.astype(jnp.float32), axis=1, keepdims=True)
        table = jnp.where(lanes == n, row_max[n] + jnp.log2(total), table)
        table = jnp.where(lanes == HEADS + n, dot, table)
        finish.append((dot, total, sums))
    stats[1, 0] = table.T[:8]
    swap(STATS).start()
    spread(0, STATS)
    for n in range(HEADS):
        dot, total, sums = finish[n]
        dq_out[:, columns(n)] = ((grad[n] - (dot - row_dot[n]) * sums[:, dim:]) * (scale / total)).astype(jnp.bfloat16)

    def keys_side(i, carry):
        run(second_events, i)
        s, o, a, there, related = place(i)

        @pl.when(there & (o > 0))
        def _():
            arrive(a, s, Q)
            arrive(a, s, G)
            arrive(a, s, STATS)

        @pl.when(there)
        def _():
            for n in range(HEADS):
                own_k, own_v = tiles[1, 0, K, :, columns(n)], tiles[1, 0, V, :, columns(n)]
                query, out_grad = tiles[a, s, Q, :, columns(n)], tiles[a, s, G, :, columns(n)]
                log_total = jnp.where(related, stats[a, s, n : n + 1], -NEGATIVE)
                dot = stats[a, s, HEADS + n : HEADS + n + 1]
                weights = jnp.exp2(nt(own_k, query) * to_log2 - log_total)
                inner = (weights * (nt(own_v, out_grad) - dot)).astype(jnp.bfloat16)
                value_acc[n] += nn(weights.astype(jnp.bfloat16), out_grad)
                key_acc[n] += nn(inner, query)

        return carry

    lax.fori_loop(0, 9, keys_side, 0)

    for n in range(HEADS):
        dk_out[:, columns(n)] = (key_acc[n] * scale).astype(jnp.bfloat16)
        dv_out[:, columns(n)] = value_acc[n].astype(jnp.bfloat16)

    for u in (K, V, Q, G, STATS):
        swap(u).wait_send()
        for s in range(2):
            to_chip(s, u).wait_send()
            off_chip(s, u).wait_send()

        @pl.when(z_to)
        def _():
            along_z(u).wait_send()

        @pl.when(z_from)
        def _():
            to_chip(2, u).wait_send()
            off_chip(2, u).wait_send()


def shards(queries, key_states, value_states, out_grad, clip_start):
    rows, channels = queries.shape[-2:]
    dim = channels // HEADS
    flat = [x.reshape(rows, channels) for x in (queries, key_states, value_states, out_grad)]
    vmem = pl.BlockSpec(memory_space=pltpu.VMEM)
    anywhere = pl.BlockSpec(memory_space=pl.ANY)
    outs = pl.pallas_call(
        kernel,
        out_shape=[jax.ShapeDtypeStruct((rows, channels), jnp.bfloat16)] * 4,
        in_specs=[pl.BlockSpec(memory_space=pltpu.SMEM)] + [anywhere] * 4,
        out_specs=[vmem] * 4,
        scratch_shapes=[
            pltpu.VMEM((3, 3, 4, rows, channels), jnp.bfloat16),
            pltpu.VMEM((3, 3, 8, rows), jnp.float32),
            pltpu.VMEM((HEADS, rows, 2 * dim), jnp.float32),
            pltpu.VMEM((HEADS, rows, dim), jnp.float32),
            pltpu.VMEM((HEADS, rows, 1), jnp.float32),
            pltpu.VMEM((HEADS, rows, 1), jnp.float32),
            pltpu.VMEM((HEADS, rows, 1), jnp.float32),
            pltpu.VMEM((HEADS, rows, dim), jnp.float32),
            pltpu.VMEM((HEADS, rows, dim), jnp.float32),
            pltpu.SemaphoreType.DMA((4,)),
            pltpu.SemaphoreType.DMA((5,)),
            pltpu.SemaphoreType.DMA((5,)),
            pltpu.SemaphoreType.DMA((5,)),
            pltpu.SemaphoreType.DMA((5,)),
            pltpu.SemaphoreType.DMA((2, 3, 5)),
            pltpu.SemaphoreType.DMA((3, 3, 5)),
        ],
        compiler_params=pltpu.CompilerParams(
            collective_id=0, has_side_effects=True, vmem_limit_bytes=48 * 2**20
        ),
        name="tile_attention",
    )(clip_start, *flat)
    return tuple(x.reshape(queries.shape) for x in outs)


def solution(mesh):
    spec = P("tm", "height", None, None, None)
    return jax.shard_map(
        shards, mesh=mesh, in_specs=(spec,) * 4 + (P(),), out_specs=(spec,) * 4, check_vma=False
    )
```

time: 173 us -> 74.8 us (0.43)
  the two profiles are of different devices: /device:TPU:6 before, /device:TPU:34 now
where the time goes in v1:
time: 74.8 us; the launch traced here: 74.5 us
  Pallas kernels  66.8 us (89%)
  local copies, waits for them, and re-layouts  6.41 us (9%)
  between operations  1.3 us (2%)
    pallas_call x1, Pallas kernels, shards(): pl.pallas_call(kernel, out_shape=[jax.ShapeDtypeStruct((rows, channels),...  66.8 us
    unnamed x12, local copies, waits for them, and re-layouts  6.41 us

profile of v1, /device:TPU:34, one launch (start us, length us, event | category | flops | bytes accessed | tf_op | source)
XLA Modules:
  0.0 74.5 jit_solution(15644967648624353593)
XLA Ops:
  1.3 0.0 copy-start
  1.3 0.9 %copy-done = bf16[1,1,1,384,256]{4,3,2,1,0:T(8,128)(2,1)S(1)} copy-done((bf16[1,1,1,384,256]{4,3,2,1,0:T(8,128)(2,1)S(1)}, bf16[1,1,1,384,256]{4,3,2,1,0:T(8,128)(2,1)}, u32[]{:S(2)}) %copy-start) | copy-done | bytes 196632
  2.2 0.0 copy-start.1
  2.2 0.9 %copy-done.1 = bf16[1,1,1,384,256]{4,3,2,1,0:T(8,128)(2,1)S(1)} copy-done((bf16[1,1,1,384,256]{4,3,2,1,0:T(8,128)(2,1)S(1)}, bf16[1,1,1,384,256]{4,3,2,1,0:T(8,128)(2,1)}, u32[]{:S(2)}) %copy-start.1) | copy-done | bytes 196632
  3.1 0.0 copy-start.2
  3.1 0.9 %copy-done.2 = bf16[1,1,1,384,256]{4,3,2,1,0:T(8,128)(2,1)S(1)} copy-done((bf16[1,1,1,384,256]{4,3,2,1,0:T(8,128)(2,1)S(1)}, bf16[1,1,1,384,256]{4,3,2,1,0:T(8,128)(2,1)}, u32[]{:S(2)}) %copy-start.2) | copy-done | bytes 196632
  4.1 0.0 copy-start.3
  4.1 0.9 %copy-done.3 = bf16[1,1,1,384,256]{4,3,2,1,0:T(8,128)(2,1)S(1)} copy-done((bf16[1,1,1,384,256]{4,3,2,1,0:T(8,128)(2,1)S(1)}, bf16[1,1,1,384,256]{4,3,2,1,0:T(8,128)(2,1)}, u32[]{:S(2)}) %copy-start.3) | copy-done | bytes 196632
  5.0 66.8 %tile_attention.1 = (bf16[384,256]{1,0:T(8,128)(2,1)S(1)}, bf16[384,256]{1,0:T(8,128)(2,1)S(1)}, bf16[384,256]{1,0:T(8,128)(2,1)S(1)}, bf16[384,256]{1,0:T(8,128)(2,1)S(1)}) custom-call(s32[1]{0:T(128)S(6)} %copy.13.clip_ref, bf16[384,256]{1,0:T(8,128)(2,1)S(1)} %bitcast.12, bf16[384,256]{1,0:T(8,128)(2,1)S(1)} %bitcast.13, bf16[384,256]{1,0:T(8,128)(2,1)S(1)} %bitcast.14, ...), custom_call_target="tpu_custom_call" | custom-call | tf_op jit(solution)/shard_map/tile_attention/pallas_call | solution.py:290
  71.8 0.7 copy.14
  72.5 0.7 copy.15
  73.2 0.7 copy.16
  73.9 0.7 copy.17
Async XLA Ops:
  1.3 0.9 %copy-start = (bf16[1,1,1,384,256]{4,3,2,1,0:T(8,128)(2,1)S(1)}, bf16[1,1,1,384,256]{4,3,2,1,0:T(8,128)(2,1)}, u32[]{:S(2)}) copy-start(bf16[1,1,1,384,256]{4,3,2,1,0:T(8,128)(2,1)} %param.5) | copy-start | bytes 589828
  2.2 0.9 %copy-start.1 = (bf16[1,1,1,384,256]{4,3,2,1,0:T(8,128)(2,1)S(1)}, bf16[1,1,1,384,256]{4,3,2,1,0:T(8,128)(2,1)}, u32[]{:S(2)}) copy-start(bf16[1,1,1,384,256]{4,3,2,1,0:T(8,128)(2,1)} %param.6) | copy-start | bytes 589828
  3.1 0.9 %copy-start.2 = (bf16[1,1,1,384,256]{4,3,2,1,0:T(8,128)(2,1)S(1)}, bf16[1,1,1,384,256]{4,3,2,1,0:T(8,128)(2,1)}, u32[]{:S(2)}) copy-start(bf16[1,1,1,384,256]{4,3,2,1,0:T(8,128)(2,1)} %param.7) | copy-start | bytes 589828
  4.1 0.9 %copy-start.3 = (bf16[1,1,1,384,256]{4,3,2,1,0:T(8,128)(2,1)S(1)}, bf16[1,1,1,384,256]{4,3,2,1,0:T(8,128)(2,1)}, u32[]{:S(2)}) copy-start(bf16[1,1,1,384,256]{4,3,2,1,0:T(8,128)(2,1)} %param.8) | copy-start | bytes 589828

commit v2 on v1

--- a/solution.py
+++ b/solution.py
@@ -24,7 +24,7 @@
 
 def kernel(
     clip_ref, q_in, k_in, v_in, g_in, att_out, dq_out, dk_out, dv_out,
-    tiles, stats, acc, grad, row_max, row_sum, row_dot, key_acc, value_acc,
+    tiles, stats, out_grad_t, acc, grad, row_max, row_sum, row_dot, key_acc, value_acc,
     local_sem, swap_send, swap_recv, z_send, z_recv, tm_send, tm_recv,
 ):
     t = lax.axis_index("tm")
@@ -155,6 +155,9 @@
     row_max[...] = jnp.full(row_max.shape, NEGATIVE, jnp.float32)
     for ref in (acc, grad, row_sum, row_dot, key_acc, value_acc):
         ref[...] = jnp.zeros(ref.shape, ref.dtype)
+    stats[1, 0] = jnp.zeros(stats.shape[2:], jnp.float32)
+    for n in range(HEADS):
+        out_grad_t[n] = tiles[1, 0, G, :, columns(n)].astype(jnp.float32).T
 
     first_events = {
         1: [(on_relay, 0, K)],
@@ -191,49 +194,54 @@
 
         @pl.when(there)
         def _():
-            for n in range(HEADS):
-                own_q, own_g = tiles[1, 0, Q, :, columns(n)], tiles[1, 0, G, :, columns(n)]
-                key, value = tiles[a, s, K, :, columns(n)], tiles[a, s, V, :, columns(n)]
-                scores = nt(own_q, key)
-                top = jnp.where(related, jnp.max(scores, axis=1, keepdims=True) * to_log2, NEGATIVE)
+            heads = range(HEADS)
+            key = [tiles[a, s, K, :, columns(n)] for n in heads]
+            value = [tiles[a, s, V, :, columns(n)] for n in heads]
+            scores = [nt(key[n], tiles[1, 0, Q, :, columns(n)]) for n in heads]
+            grad_weights = [nt(value[n], tiles[1, 0, G, :, columns(n)]) for n in heads]
+            key_t = [key[n].T for n in heads]
+            both_t = [jnp.concatenate([value[n].T, key_t[n]], axis=0) for n in heads]
+            fades, raised, totals, dots = [], [], [], []
+            for n in heads:
+                top = jnp.where(related, jnp.max(scores[n], axis=0, keepdims=True) * to_log2, NEGATIVE)
                 old_max = row_max[n]
                 new_max = jnp.maximum(old_max, top)
-                fade = jnp.exp2(old_max - new_max)
-                raised = jnp.exp2(scores * to_log2 - jnp.where(related, new_max, -NEGATIVE))
-                total = row_sum[n] * fade + jnp.sum(raised, axis=1, keepdims=True)
+                fades.append(jnp.exp2(old_max - new_max))
+                raised.append(jnp.exp2(scores[n] * to_log2 - jnp.where(related, new_max, -NEGATIVE)))
+                totals.append(row_sum[n] * fades[n] + jnp.sum(raised[n], axis=0, keepdims=True))
+                row_max[n] = new_max
+                row_sum[n] = totals[n]
+            for n in heads:
                 old = acc[n]
-                new = old * fade + nn(raised.astype(jnp.bfloat16), jnp.concatenate([value, key], axis=1))
-                old_dot = row_dot[n]
-                dot = jnp.sum(own_g.astype(jnp.float32) * new[:, :dim], axis=1, keepdims=True) / total
-                inner = (raised * (nt(own_g, value) - dot)).astype(jnp.bfloat16)
-                grad[n] = (grad[n] - (dot - old_dot) * old[:, dim:]) * fade + nn(inner, key)
+                new = old * fades[n] + nn(both_t[n], raised[n].astype(jnp.bfloat16))
+                dots.append(jnp.sum(out_grad_t[n] * new[:dim], axis=0, keepdims=True) / totals[n])
+                grad[n] = (grad[n] - (dots[n] - row_dot[n]) * old[dim:]) * fades[n]
                 acc[n] = new
-                row_max[n] = new_max
-                row_sum[n] = total
-                row_dot[n] = dot
+                row_dot[n] = dots[n]
+            for n in heads:
+                inner = (raised[n] * (grad_weights[n] - dots[n])).astype(jnp.bfloat16)
+                grad[n] += nn(key_t[n], inner)
 
         return carry
 
     lax.fori_loop(0, 9, queries_side, 0)
 
-    lanes = lax.broadcasted_iota(jnp.int32, (q_in.shape[0], 128), 1)
-    table = jnp.zeros((q_in.shape[0], 128), jnp.float32)
     finish = []
     for n in range(HEADS):
         total = row_sum[n]
         sums = acc[n]
-        attended = (sums[:, :dim] / total).astype(jnp.bfloat16)
-        att_out[:, columns(n)] = attended
-        dot = jnp.sum(tiles[1, 0, G, :, columns(n)].astype(jnp.float32) * attended.astype(jnp.float32), axis=1, keepdims=True)
-        table = jnp.where(lanes == n, row_max[n] + jnp.log2(total), table)
-        table = jnp.where(lanes == HEADS + n, dot, table)
-        finish.append((dot, total, sums))
-    stats[1, 0] = table.T[:8]
+        attended = (sums[:dim] / total).astype(jnp.bfloat16).astype(jnp.float32)
+        dot = jnp.sum(out_grad_t[n] * attended, axis=0, keepdims=True)
+        stats[1, 0, n : n + 1] = row_max[n] + jnp.log2(total)
+        stats[1, 0, HEADS + n : HEADS + n + 1] = dot
+        finish.append((dot, total, sums, attended))
     swap(STATS).start()
     spread(0, STATS)
     for n in range(HEADS):
-        dot, total, sums = finish[n]
-        dq_out[:, columns(n)] = ((grad[n] - (dot - row_dot[n]) * sums[:, dim:]) * (scale / total)).astype(jnp.bfloat16)
+        dot, total, sums, attended = finish[n]
+        att_out[:, columns(n)] = attended.T.astype(jnp.bfloat16)
+        own_grad = (grad[n] - (dot - row_dot[n]) * sums[dim:]) * (scale / total)
+        dq_out[:, columns(n)] = own_grad.T.astype(jnp.bfloat16)
 
     def keys_side(i, carry):
         run(second_events, i)
@@ -281,6 +289,15 @@
             off_chip(2, u).wait_send()
 
 
+def write_out(*refs):
+    sources, targets, sems = refs[:4], refs[4:8], refs[8]
+    copies = [pltpu.make_async_copy(sources[i], targets[i], sems.at[i]) for i in range(4)]
+    for copy in copies:
+        copy.start()
+    for copy in copies:
+        copy.wait()
+
+
 def shards(queries, key_states, value_states, out_grad, clip_start):
     rows, channels = queries.shape[-2:]
     dim = channels // HEADS
@@ -290,16 +307,17 @@
     outs = pl.pallas_call(
         kernel,
         out_shape=[jax.ShapeDtypeStruct((rows, channels), jnp.bfloat16)] * 4,
-        in_specs=[pl.BlockSpec(memory_space=pltpu.SMEM)] + [anywhere] * 4,
+        in_specs=[pl.BlockSpec(memory_space=pltpu.SMEM)] + [pl.BlockSpec(memory_space=pltpu.HBM)] * 4,
         out_specs=[vmem] * 4,
         scratch_shapes=[
             pltpu.VMEM((3, 3, 4, rows, channels), jnp.bfloat16),
             pltpu.VMEM((3, 3, 8, rows), jnp.float32),
-            pltpu.VMEM((HEADS, rows, 2 * dim), jnp.float32),
-            pltpu.VMEM((HEADS, rows, dim), jnp.float32),
-            pltpu.VMEM((HEADS, rows, 1), jnp.float32),
-            pltpu.VMEM((HEADS, rows, 1), jnp.float32),
-            pltpu.VMEM((HEADS, rows, 1), jnp.float32),
+            pltpu.VMEM((HEADS, dim, rows), jnp.float32),
+            pltpu.VMEM((HEADS, 2 * dim, rows), jnp.float32),
+            pltpu.VMEM((HEADS, dim, rows), jnp.float32),
+            pltpu.VMEM((HEADS, 1, rows), jnp.float32),
+            pltpu.VMEM((HEADS, 1, rows), jnp.float32),
+            pltpu.VMEM((HEADS, 1, rows), jnp.float32),
             pltpu.VMEM((HEADS, rows, dim), jnp.float32),
             pltpu.VMEM((HEADS, rows, dim), jnp.float32),
             pltpu.SemaphoreType.DMA((4,)),
@@ -315,6 +333,14 @@
         ),
         name="tile_attention",
     )(clip_start, *flat)
+    outs = pl.pallas_call(
+        write_out,
+        out_shape=[jax.ShapeDtypeStruct((rows, channels), jnp.bfloat16)] * 4,
+        in_specs=[anywhere] * 4,
+        out_specs=[anywhere] * 4,
+        scratch_shapes=[pltpu.SemaphoreType.DMA((4,))],
+        name="write_out",
+    )(*outs)
     return tuple(x.reshape(queries.shape) for x in outs)
 
 

time: 74.8 us -> 94.8 us (1.27)
  the two profiles are of different devices: /device:TPU:34 before, /device:TPU:6 now
where the time goes in v2:
time: 94.8 us; the launch traced here: 93.5 us
  Pallas kernels  85.8 us (91%)
  local copies, waits for them, and re-layouts  6.37 us (7%)
  between operations  1.31 us (1%)
    pallas_call x1, Pallas kernels, shards(): pl.pallas_call(kernel, out_shape=[jax.ShapeDtypeStruct((rows, channels),...  60.9 us
    pallas_call x1, Pallas kernels, shards(): pl.pallas_call(write_out, out_shape=[jax.ShapeDtypeStruct((rows, channels...  25 us
    unnamed x16, local copies, waits for them, and re-layouts  6.37 us

profile of v2, /device:TPU:6, one launch (start us, length us, event | category | flops | bytes accessed | tf_op | source)
XLA Modules:
  0.0 93.5 jit_solution(16511376906938695843)
XLA Ops:
  1.3 0.0 copy-start
  1.3 0.9 copy-done
  2.2 0.0 copy-start.1
  2.2 0.9 copy-done.1
  3.1 0.0 copy-start.2
  3.1 0.9 copy-done.2
  4.1 0.0 copy-start.3
  4.1 0.9 copy-done.3
  5.0 60.9 %tile_attention.1 = (bf16[384,256]{1,0:T(8,128)(2,1)S(1)}, bf16[384,256]{1,0:T(8,128)(2,1)S(1)}, bf16[384,256]{1,0:T(8,128)(2,1)S(1)}, bf16[384,256]{1,0:T(8,128)(2,1)S(1)}) custom-call(s32[1]{0:T(128)S(6)} %copy.9.clip_ref, bf16[384,256]{1,0:T(8,128)(2,1)S(1)} %bitcast.8, bf16[384,256]{1,0:T(8,128)(2,1)S(1)} %bitcast.9, bf16[384,256]{1,0:T(8,128)(2,1)S(1)} %bitcast.10, ...), custom_call_target="tpu_custom_call" | custom-call | tf_op jit(solution)/shard_map/tile_attention/pallas_call | solution.py:307
  65.9 0.0 copy-start.4
  65.9 0.7 copy-done.4
  66.5 0.0 copy-start.5
  66.5 0.7 copy-done.5
  67.2 0.0 copy-start.6
  67.2 0.7 copy-done.6
  67.9 0.0 copy-start.7
  67.9 0.7 copy-done.7
  68.6 25.0 %write_out.1 = (bf16[384,256]{1,0:T(8,128)(2,1)}, bf16[384,256]{1,0:T(8,128)(2,1)}, bf16[384,256]{1,0:T(8,128)(2,1)}, bf16[384,256]{1,0:T(8,128)(2,1)}) custom-call(bf16[384,256]{1,0:T(8,128)(2,1)} %copy-done.4, bf16[384,256]{1,0:T(8,128)(2,1)} %copy-done.5, bf16[384,256]{1,0:T(8,128)(2,1)} %copy-done.6, bf16[384,256]{1,0:T(8,128)(2,1)} %copy-done.7), custom_call_target="tpu_custom_call" | custom-call | tf_op jit(solution)/shard_map/write_out/pallas_call | solution.py:336
Async XLA Ops:
  1.3 0.9 copy-start
  2.2 0.9 copy-start.1
  3.1 0.9 copy-start.2
  4.1 0.9 copy-start.3
  65.9 0.7 copy-start.4
  66.5 0.7 copy-start.5
  67.2 0.7 copy-start.6
  67.9 0.7 copy-start.7

commit v3 on v1

v3 whole, which is shorter than its diff:
```python
import jax
import jax.numpy as jnp
from jax import lax
from jax.experimental import pallas as pl
from jax.experimental.pallas import tpu as pltpu
from jax.sharding import PartitionSpec as P

HEADS = 2
LOG2E = 1.4426950408889634
NEGATIVE = -1e30
MESH = pl.DeviceIdType.MESH
QUERIES, FINISH, KEYS, NOTHING = range(4)
K, V, Q, G = range(4)
PIECES = 2
EARLY = 2 * PIECES
CHUNKS = 4 * PIECES


def nt(left, right):
    return lax.dot_general(left, right, (((1,), (1,)), ((), ())), preferred_element_type=jnp.float32)


def nn(left, right):
    return jnp.dot(left, right, preferred_element_type=jnp.float32)


def kernel(
    clip_ref, q_in, k_in, v_in, g_in, out_ref,
    tiles, stats, out_grad_t, acc, grad, row_max, row_sum, row_dot, key_acc, value_acc,
    local_sem, swap_send, swap_recv, z_send, z_recv, tm_send, tm_recv, side_send, stats_send, stats_recv,
):
    t = lax.axis_index("tm")
    h = lax.axis_index("height")
    core, odd, z = t % 2, h % 2, h // 2
    dim = q_in.shape[-1] // HEADS
    scale = dim ** (-0.5)
    to_log2 = scale * LOG2E

    copies = [pltpu.make_async_copy(ref, tiles.at[1, 0, u], local_sem.at[u]) for u, ref in enumerate((k_in, v_in, q_in, g_in))]
    for copy in copies:
        copy.start()

    first, last, left, right = t == 0, t == 15, t == 7, t == 8
    relay, bound = first | last, left | right
    other = h + 1 - 2 * odd
    chip_dev = (t + 1 - 2 * core, h)
    z_to = jnp.where(odd == 0, z < 3, z > 0)
    z_from = jnp.where(odd == 0, z > 0, z < 3)
    z_dst = (t, h + 2 - 4 * odd)
    z_src = (t, h - 2 + 4 * odd)
    chip_there = jnp.where(core == 0, 0, 2)
    chip_here = 2 - chip_there
    off_here = chip_there
    near = jnp.where(core == 1, t + 1, t - 1)
    near_slot = jnp.where(core == 1, 0, 2)

    def pick(at_left, at_right, at_last, at_first, usual):
        return jnp.where(left, at_left, jnp.where(right, at_right, jnp.where(last, at_last, jnp.where(first, at_first, usual))))

    own_dev, own_slot = pick(0, 15, 7, 8, near), pick(0, 2, 2, 0, near_slot)
    off_from = pick(1, 1, 2, 0, 1)

    neighbours = [(dt, dh) for dt in (-1, 0, 1) for dh in (-1, 0, 1) if dt or dh]

    def exists(dt, dh):
        return (t + dt >= 0) & (t + dt <= 15) & (h + dh >= 0) & (h + dh <= 7)

    barrier = pltpu.get_barrier_semaphore()

    def greet(frame, row):
        pl.semaphore_signal(barrier, inc=1, device_id=(frame, row), device_id_type=MESH)

    targets = (relay | bound).astype(jnp.int32) + z_to.astype(jnp.int32)
    for dt, dh in neighbours:
        targets = targets + exists(dt, dh).astype(jnp.int32)

        @pl.when(exists(dt, dh))
        def _():
            greet(t + dt, h + dh)

    @pl.when(relay | bound)
    def _():
        greet(pick(15, 0, 8, 7, 0), h)

    @pl.when(z_from)
    def _():
        greet(*z_src)

    pl.semaphore_wait(barrier, targets)

    def part(a, s, k):
        u, piece = k // PIECES, k % PIECES
        size = tiles.shape[3] // PIECES
        return tiles.at[a, s, u, pl.ds(piece * size, size)]

    def remote(src, dst, send, recv, device):
        return pltpu.make_async_remote_copy(
            src_ref=src, dst_ref=dst, send_sem=send, recv_sem=recv, device_id=device, device_id_type=MESH
        )

    def swap(k):
        return remote(part(1, 0, k), part(1, 1, k), swap_send.at[k], swap_recv.at[k], (t, other))

    def along_z(k):
        return remote(part(1, 1, k), part(1, 2, k), z_send.at[k], z_recv.at[k], z_dst)

    def side_z(k):
        return remote(part(off_here, 1, k), part(off_here, 2, k), side_send.at[k], tm_recv.at[off_here, 2, k], z_dst)

    def to_chip(s, k):
        return remote(part(1, s, k), part(chip_there, s, k), tm_send.at[0, s, k], tm_recv.at[chip_there, s, k], chip_dev)

    def off_chip(s, k):
        frame, slot = (near, near_slot) if s else (own_dev, own_slot)
        return remote(part(off_from, s, k), part(slot, s, k), tm_send.at[1, s, k], tm_recv.at[slot, s, k], (frame, h))

    def arrive(a, s, k):
        remote(part(1, s, k), part(a, s, k), tm_send.at[0, s, k], tm_recv.at[a, s, k], chip_dev).wait_recv()

    def row_stats(dt, dh):
        a = 1 - dt
        s = jnp.where(odd == (dh + 1) // 2, 2, 1) * dh * dh
        return remote(stats.at[1, 0], stats.at[a, s], stats_send.at[a, dh + 1], stats_recv.at[a, s], (t + dt, h + dh))

    def spread(s, k):
        @pl.when(~(relay | bound) if s == 2 else ~relay)
        def _():
            off_chip(s, k).start()

        to_chip(s, k).start()

    def begin(k):
        swap(k).start()
        spread(0, k)

    def on_swap(k):
        swap(k).wait_recv()

        @pl.when(z_to)
        def _():
            along_z(k).start()

        spread(1, k)

    def on_z(k):
        @pl.when(z_from)
        def _():
            along_z(k).wait_recv()
            spread(2, k)

    def on_relay(k):
        arrive(off_here, 0, k)
        off_chip(0, k).start()

    def on_side(k):
        arrive(off_here, 1, k)

        @pl.when(z_to)
        def _():
            side_z(k).start()

    for copy in copies:
        copy.wait()
    for k in range(4):
        begin(k)

    clip = clip_ref[0]

    def columns(n):
        return slice(n * dim, (n + 1) * dim)

    row_max[...] = jnp.full(row_max.shape, NEGATIVE, jnp.float32)
    for ref in (acc, grad, row_sum, row_dot, key_acc, value_acc):
        ref[...] = jnp.zeros(ref.shape, ref.dtype)
    stats[1, 0] = jnp.zeros(stats.shape[2:], jnp.float32)
    for n in range(HEADS):
        out_grad_t[n] = tiles[1, 0, G, :, columns(n)].astype(jnp.float32).T

    EVENTS = (
        {
            2: [(on_swap, 0)],
            3: [(on_swap, 1), (on_z, 0), (on_swap, 2), (on_swap, 3)],
            4: [(begin, 4), (begin, 5), (on_z, 1)],
            5: [(on_z, 2)],
            6: [(on_z, 3)],
            7: [(begin, 6), (begin, 7), (on_swap, 4)],
            8: [(on_swap, 5)],
            9: [(on_z, 4), (on_swap, 6)],
            10: [(on_z, 5), (on_swap, 7)],
            12: [(on_z, 6)],
            16: [(on_z, 7)],
        },
        {
            2: [(on_swap, 0), (on_swap, 1), (on_z, 0), (on_swap, 2), (on_z, 1), (on_swap, 3)],
            3: [(begin, 4), (begin, 5), (on_side, 0)],
            4: [(on_side, 1), (on_z, 2), (on_side, 2)],
            5: [(on_z, 3), (begin, 6), (begin, 7), (on_side, 3)],
            6: [(on_swap, 4)],
            7: [(on_swap, 5)],
            9: [(on_swap, 6)],
            10: [(on_z, 4), (on_swap, 7), (on_z, 5)],
            11: [(on_side, 4)],
            12: [(on_side, 5), (on_z, 6)],
            13: [(on_side, 6), (on_z, 7)],
            14: [(on_side, 7)],
        },
        {
            2: [(on_relay, 0), (on_relay, 1), (on_swap, 0), (on_relay, 2), (on_relay, 3), (on_swap, 1), (on_z, 0), (on_swap, 2), (on_z, 1), (on_swap, 3), (begin, 4), (begin, 5)],
            4: [(on_z, 2), (on_relay, 4), (on_z, 3)],
            5: [(begin, 6), (begin, 7), (on_relay, 5)],
            6: [(on_swap, 4)],
            7: [(on_swap, 5)],
            8: [(on_relay, 6), (on_relay, 7), (on_z, 4), (on_z, 5), (on_swap, 6)],
            9: [(on_swap, 7)],
            10: [(on_z, 6)],
            11: [(on_z, 7)],
        },
    )
    KIND = (
        (0, 0, 0, 0, 0, 0, 0, 0, 0, 1, 2, 2, 2, 2, 2, 2, 2, 2, 2, 3),
        (0, 0, 0, 0, 0, 0, 0, 0, 0, 1, 2, 2, 2, 2, 2, 2, 2, 2, 2, 3),
        (0, 0, 0, 0, 0, 0, 1, 2, 2, 2, 2, 2, 2, 3, 3, 3, 3, 3, 3, 3),
    )
    ROW = (
        (0, 0, 0, 1, 1, 1, 2, 2, 2, 0, 0, 0, 0, 1, 1, 1, 2, 2, 2, 0),
        (0, 0, 1, 1, 0, 2, 2, 1, 2, 0, 0, 0, 1, 0, 1, 2, 2, 1, 2, 0),
        (0, 0, 1, 1, 2, 2, 0, 0, 0, 1, 1, 2, 2, 0, 0, 0, 0, 0, 0, 0),
    )
    FRAME = (
        (0, 1, 2, 0, 1, 2, 0, 1, 2, 0, 0, 1, 2, 0, 1, 2, 0, 1, 2, 0),
        (0, 1, 0, 1, 2, 0, 1, 2, 2, 0, 0, 1, 0, 2, 1, 0, 1, 2, 2, 0),
        (0, 1, 0, 1, 0, 1, 0, 0, 1, 0, 1, 0, 1, 0, 0, 0, 0, 0, 0, 0),
    )
    STEPS = 20

    def choose(step, tables):
        def at(table):
            value = jnp.int32(table[-1])
            for i in range(len(table) - 2, -1, -1):
                value = jnp.where(step == i, table[i], value)
            return value

        return jnp.where(relay, at(tables[2]), jnp.where(bound, at(tables[1]), at(tables[0])))

    def queries_side(a, s, related):
        heads = range(HEADS)
        key = [tiles[a, s, K, :, columns(n)] for n in heads]
        value = [tiles[a, s, V, :, columns(n)] for n in heads]
        scores = [nt(key[n], tiles[1, 0, Q, :, columns(n)]) for n in heads]
        grad_weights = [nt(value[n], tiles[1, 0, G, :, columns(n)]) for n in heads]
        key_t = [key[n].T for n in heads]
        both_t = [jnp.concatenate([value[n].T, key_t[n]], axis=0) for n in heads]
        fades, raised, totals, dots = [], [], [], []
        for n in heads:
            top = jnp.where(related, jnp.max(scores[n], axis=0, keepdims=True) * to_log2, NEGATIVE)
            old_max = row_max[n]
            new_max = jnp.maximum(old_max, top)
            fades.append(jnp.exp2(old_max - new_max))
            raised.append(jnp.exp2(scores[n] * to_log2 - jnp.where(related, new_max, -NEGATIVE)))
            totals.append(row_sum[n] * fades[n] + jnp.sum(raised[n], axis=0, keepdims=True))
            row_max[n] = new_max
            row_sum[n] = totals[n]
        for n in heads:
            old = acc[n]
            new = old * fades[n] + nn(both_t[n], raised[n].astype(jnp.bfloat16))
            dots.append(jnp.sum(out_grad_t[n] * new[:dim], axis=0, keepdims=True) / totals[n])
            grad[n] = (grad[n] - (dots[n] - row_dot[n]) * old[dim:]) * fades[n]
            acc[n] = new
            row_dot[n] = dots[n]
        for n in heads:
            inner = (raised[n] * (grad_weights[n] - dots[n])).astype(jnp.bfloat16)
            grad[n] += nn(key_t[n], inner)

    def finish_queries():
        finish = []
        for n in range(HEADS):
            total = row_sum[n]
            sums = acc[n]
            attended = (sums[:dim] / total).astype(jnp.bfloat16).astype(jnp.float32)
            dot = jnp.sum(out_grad_t[n] * attended, axis=0, keepdims=True)
            stats[1, 0, n : n + 1] = row_max[n] + jnp.log2(total)
            stats[1, 0, HEADS + n : HEADS + n + 1] = dot
            finish.append((dot, total, sums, attended))
        for dt, dh in neighbours:
            @pl.when(exists(dt, dh))
            def _():
                row_stats(dt, dh).start()

        for n in range(HEADS):
            dot, total, sums, attended = finish[n]
            out_ref[0, :, columns(n)] = attended.T.astype(jnp.bfloat16)
            own_grad = (grad[n] - (dot - row_dot[n]) * sums[dim:]) * (scale / total)
            out_ref[1, :, columns(n)] = own_grad.T.astype(jnp.bfloat16)

    def keys_side(a, s, related):
        for n in range(HEADS):
            own_k, own_v = tiles[1, 0, K, :, columns(n)], tiles[1, 0, V, :, columns(n)]
            query, out_grad = tiles[a, s, Q, :, columns(n)], tiles[a, s, G, :, columns(n)]
            log_total = jnp.where(related, stats[a, s, n : n + 1], -NEGATIVE)
            dot = stats[a, s, HEADS + n : HEADS + n + 1]
            weights = jnp.exp2(nt(own_k, query) * to_log2 - log_total)
            inner = (weights * (nt(own_v, out_grad) - dot)).astype(jnp.bfloat16)
            value_acc[n] += nn(weights.astype(jnp.bfloat16), out_grad)
            key_acc[n] += nn(inner, query)

    def do_step(step, carry):
        for mine, events in zip((~(relay | bound), bound, relay), EVENTS):
            for at, entries in events.items():
                @pl.when(mine & (step == at))
                def _():
                    for entry in entries:
                        entry[0](*entry[1:])

        kind, s, o = choose(step, KIND), choose(step, ROW), choose(step, FRAME)
        a = jnp.where(o == 0, 1, jnp.where(o == 1, chip_here, off_here))
        there = ((s < 2) | z_from) & ((o < 2) | ~relay)
        related = ((t + a - 1) >= clip) == (t >= clip)
        waits = (o > 0) & ~(bound & (o == 2) & (s == 1))

        @pl.when(there & (kind == QUERIES))
        def _():
            @pl.when(waits)
            def _():
                for k in range(EARLY):
                    arrive(a, s, k)

            queries_side(a, s, related)

        @pl.when(kind == FINISH)
        def _():
            finish_queries()

        @pl.when(there & (kind == KEYS))
        def _():
            @pl.when(waits)
            def _():
                for k in range(EARLY, CHUNKS):
                    arrive(a, s, k)

            @pl.when((s > 0) | (o > 0))
            def _():
                remote(stats.at[1, 0], stats.at[a, s], stats_send.at[1, 1], stats_recv.at[a, s], chip_dev).wait_recv()

            keys_side(a, s, related)

        return carry

    lax.fori_loop(0, STEPS, do_step, 0)

    for n in range(HEADS):
        out_ref[2, :, columns(n)] = (key_acc[n] * scale).astype(jnp.bfloat16)
        out_ref[3, :, columns(n)] = value_acc[n].astype(jnp.bfloat16)

    for k in range(CHUNKS):
        to_chip(0, k).wait_send()
        off_chip(0, k).wait_send()
        to_chip(1, k).wait_send()

        @pl.when(~relay)
        def _():
            off_chip(1, k).wait_send()

        swap(k).wait_send()

        @pl.when(z_to)
        def _():
            along_z(k).wait_send()

        @pl.when(z_to & bound)
        def _():
            side_z(k).wait_send()

        @pl.when(z_from)
        def _():
            to_chip(2, k).wait_send()

        @pl.when(z_from & ~(relay | bound))
        def _():
            off_chip(2, k).wait_send()

    for dt, dh in neighbours:
        @pl.when(exists(dt, dh))
        def _():
            row_stats(dt, dh).wait_send()


def shards(queries, key_states, value_states, out_grad, clip_start):
    rows, channels = queries.shape[-2:]
    dim = channels // HEADS
    flat = [x.reshape(rows, channels) for x in (queries, key_states, value_states, out_grad)]
    vmem = pl.BlockSpec(memory_space=pltpu.VMEM)
    outs = pl.pallas_call(
        kernel,
        out_shape=jax.ShapeDtypeStruct((4, rows, channels), jnp.bfloat16),
        in_specs=[pl.BlockSpec(memory_space=pltpu.SMEM)] + [pl.BlockSpec(memory_space=pltpu.HBM)] * 4,
        out_specs=vmem,
        scratch_shapes=[
            pltpu.VMEM((3, 3, 4, rows, channels), jnp.bfloat16),
            pltpu.VMEM((3, 3, 8, rows), jnp.float32),
            pltpu.VMEM((HEADS, dim, rows), jnp.float32),
            pltpu.VMEM((HEADS, 2 * dim, rows), jnp.float32),
            pltpu.VMEM((HEADS, dim, rows), jnp.float32),
            pltpu.VMEM((HEADS, 1, rows), jnp.float32),
            pltpu.VMEM((HEADS, 1, rows), jnp.float32),
            pltpu.VMEM((HEADS, 1, rows), jnp.float32),
            pltpu.VMEM((HEADS, rows, dim), jnp.float32),
            pltpu.VMEM((HEADS, rows, dim), jnp.float32),
            pltpu.SemaphoreType.DMA((4,)),
            pltpu.SemaphoreType.DMA((CHUNKS,)),
            pltpu.SemaphoreType.DMA((CHUNKS,)),
            pltpu.SemaphoreType.DMA((CHUNKS,)),
            pltpu.SemaphoreType.DMA((CHUNKS,)),
            pltpu.SemaphoreType.DMA((2, 3, CHUNKS)),
            pltpu.SemaphoreType.DMA((3, 3, CHUNKS)),
            pltpu.SemaphoreType.DMA((CHUNKS,)),
            pltpu.SemaphoreType.DMA((3, 3)),
            pltpu.SemaphoreType.DMA((3, 3)),
        ],
        compiler_params=pltpu.CompilerParams(
            collective_id=0, has_side_effects=True, vmem_limit_bytes=64 * 2**20
        ),
        name="tile_attention",
    )(clip_start, *flat)
    return tuple(outs[i].reshape(queries.shape) for i in range(4))


def solution(mesh):
    spec = P("tm", "height", None, None, None)
    return jax.shard_map(
        shards, mesh=mesh, in_specs=(spec,) * 4 + (P(),), out_specs=(spec,) * 4, check_vma=False
    )
```

time: 74.8 us -> 52 us (0.70)
  the two profiles are of different devices: /device:TPU:34 before, /device:TPU:6 now
where the time goes in v3:
time: 52 us; the launch traced here: 51.6 us
  Pallas kernels  48.2 us (93%)
  local copies, waits for them, and re-layouts  2.11 us (4%)
  between operations  1.29 us (2%)
    pallas_call x1, Pallas kernels, shards(): pl.pallas_call(kernel, out_shape=jax.ShapeDtypeStruct((4, rows, channels)...  48.2 us
    another operation x1, local copies, waits for them, and re-layouts, shards(): return tuple((outs[i].reshape(queries.shape) for i in range(4)))  2.11 us

profile of v3, /device:TPU:6, one launch (start us, length us, event | category | flops | bytes accessed | tf_op | source)
XLA Modules:
  0.0 51.6 jit_solution(16547994694337623251)
XLA Ops:
  1.3 48.2 %tile_attention.1 = bf16[4,384,256]{2,1,0:T(8,128)(2,1)} custom-call(s32[1]{0:T(128)S(6)} %copy.9.clip_ref, bf16[384,256]{1,0:T(8,128)(2,1)} %bitcast.12, bf16[384,256]{1,0:T(8,128)(2,1)} %bitcast.13, bf16[384,256]{1,0:T(8,128)(2,1)} %bitcast.14, bf16[384,256]{1,0:T(8,128)(2,1)} %bitcast.15), custom_call_target="tpu_custom_call" | custom-call | tf_op jit(solution)/shard_map/tile_attention/pallas_call | solution.py:392
  49.5 2.1 %slice_bitcast_fusion = (bf16[1,1,1,384,256]{4,3,2,1,0:T(8,128)(2,1)}, bf16[1,1,1,384,256]{4,3,2,1,0:T(8,128)(2,1)}, bf16[1,1,1,384,256]{4,3,2,1,0:T(8,128)(2,1)}, bf16[1,1,1,384,256]{4,3,2,1,0:T(8,128)(2,1)}) fusion(bf16[4,384,256]{2,1,0:T(8,128)(2,1)} %tile_attention.1), kind=kLoop, calls=%fused_computation | loop fusion | bytes 1572864 | tf_op jit(solution)/shard_map/reshape;squeeze | solution.py:424

commit v4 on v3

--- a/solution.py
+++ b/solution.py
@@ -27,7 +27,7 @@
 def kernel(
     clip_ref, q_in, k_in, v_in, g_in, out_ref,
     tiles, stats, out_grad_t, acc, grad, row_max, row_sum, row_dot, key_acc, value_acc,
-    local_sem, swap_send, swap_recv, z_send, z_recv, tm_send, tm_recv, side_send, stats_send, stats_recv,
+    local_sem, sent, swap_recv, z_recv, chip_recv, off_recv, stats_send, stats_recv,
 ):
     t = lax.axis_index("tm")
     h = lax.axis_index("height")
@@ -99,23 +99,27 @@
         )
 
     def swap(k):
-        return remote(part(1, 0, k), part(1, 1, k), swap_send.at[k], swap_recv.at[k], (t, other))
+        return remote(part(1, 0, k), part(1, 1, k), sent.at[0], swap_recv.at[k], (t, other))
 
     def along_z(k):
-        return remote(part(1, 1, k), part(1, 2, k), z_send.at[k], z_recv.at[k], z_dst)
+        return remote(part(1, 1, k), part(1, 2, k), sent.at[1], z_recv.at[k], z_dst)
 
     def side_z(k):
-        return remote(part(off_here, 1, k), part(off_here, 2, k), side_send.at[k], tm_recv.at[off_here, 2, k], z_dst)
+        return remote(part(off_here, 1, k), part(off_here, 2, k), sent.at[2], off_recv.at[2, k], z_dst)
 
     def to_chip(s, k):
-        return remote(part(1, s, k), part(chip_there, s, k), tm_send.at[0, s, k], tm_recv.at[chip_there, s, k], chip_dev)
+        return remote(part(1, s, k), part(chip_there, s, k), sent.at[3 + s], chip_recv.at[s, k // EARLY], chip_dev)
 
     def off_chip(s, k):
         frame, slot = (near, near_slot) if s else (own_dev, own_slot)
-        return remote(part(off_from, s, k), part(slot, s, k), tm_send.at[1, s, k], tm_recv.at[slot, s, k], (frame, h))
-
-    def arrive(a, s, k):
-        remote(part(1, s, k), part(a, s, k), tm_send.at[0, s, k], tm_recv.at[a, s, k], chip_dev).wait_recv()
+        return remote(part(off_from, s, k), part(slot, s, k), sent.at[6 + s], off_recv.at[s, k], (frame, h))
+
+    def arrive(s, k):
+        remote(part(1, s, k), part(off_here, s, k), sent.at[6], off_recv.at[s, k], chip_dev).wait_recv()
+
+    def arrive_chip(s, late):
+        both = tiles.at[chip_here, s, pl.ds(2 * late, 2)]
+        remote(both, both, sent.at[3], chip_recv.at[s, late], chip_dev).wait_recv()
 
     def row_stats(dt, dh):
         a = 1 - dt
@@ -149,11 +153,11 @@
             spread(2, k)
 
     def on_relay(k):
-        arrive(off_here, 0, k)
+        arrive(0, k)
         off_chip(0, k).start()
 
     def on_side(k):
-        arrive(off_here, 1, k)
+        arrive(1, k)
 
         @pl.when(z_to)
         def _():
@@ -180,29 +184,29 @@
         {
             2: [(on_swap, 0)],
             3: [(on_swap, 1), (on_z, 0), (on_swap, 2), (on_swap, 3)],
-            4: [(begin, 4), (begin, 5), (on_z, 1)],
+            4: [(on_z, 1), (begin, 4), (begin, 5)],
             5: [(on_z, 2)],
             6: [(on_z, 3)],
             7: [(begin, 6), (begin, 7), (on_swap, 4)],
             8: [(on_swap, 5)],
             9: [(on_z, 4), (on_swap, 6)],
             10: [(on_z, 5), (on_swap, 7)],
-            12: [(on_z, 6)],
-            16: [(on_z, 7)],
+            13: [(on_z, 6)],
+            14: [(on_z, 7)],
         },
         {
             2: [(on_swap, 0), (on_swap, 1), (on_z, 0), (on_swap, 2), (on_z, 1), (on_swap, 3)],
-            3: [(begin, 4), (begin, 5), (on_side, 0)],
-            4: [(on_side, 1), (on_z, 2), (on_side, 2)],
-            5: [(on_z, 3), (begin, 6), (begin, 7), (on_side, 3)],
-            6: [(on_swap, 4)],
-            7: [(on_swap, 5)],
-            9: [(on_swap, 6)],
-            10: [(on_z, 4), (on_swap, 7), (on_z, 5)],
-            11: [(on_side, 4)],
-            12: [(on_side, 5), (on_z, 6)],
-            13: [(on_side, 6), (on_z, 7)],
-            14: [(on_side, 7)],
+            3: [(on_z, 2), (begin, 4), (begin, 5), (on_side, 0)],
+            4: [(on_side, 1), (on_z, 3), (on_side, 2)],
+            5: [(on_side, 3)],
+            6: [(begin, 6), (begin, 7)],
+            7: [(on_swap, 4)],
+            8: [(on_swap, 5)],
+            10: [(on_swap, 6), (on_z, 4)],
+            11: [(on_z, 5), (on_swap, 7)],
+            12: [(on_side, 4), (on_side, 5)],
+            14: [(on_side, 6), (on_z, 6)],
+            15: [(on_z, 7), (on_side, 7)],
         },
         {
             2: [(on_relay, 0), (on_relay, 1), (on_swap, 0), (on_relay, 2), (on_relay, 3), (on_swap, 1), (on_z, 0), (on_swap, 2), (on_z, 1), (on_swap, 3), (begin, 4), (begin, 5)],
@@ -216,31 +220,39 @@
             11: [(on_z, 7)],
         },
     )
-    KIND = (
-        (0, 0, 0, 0, 0, 0, 0, 0, 0, 1, 2, 2, 2, 2, 2, 2, 2, 2, 2, 3),
-        (0, 0, 0, 0, 0, 0, 0, 0, 0, 1, 2, 2, 2, 2, 2, 2, 2, 2, 2, 3),
-        (0, 0, 0, 0, 0, 0, 1, 2, 2, 2, 2, 2, 2, 3, 3, 3, 3, 3, 3, 3),
-    )
-    ROW = (
-        (0, 0, 0, 1, 1, 1, 2, 2, 2, 0, 0, 0, 0, 1, 1, 1, 2, 2, 2, 0),
-        (0, 0, 1, 1, 0, 2, 2, 1, 2, 0, 0, 0, 1, 0, 1, 2, 2, 1, 2, 0),
-        (0, 0, 1, 1, 2, 2, 0, 0, 0, 1, 1, 2, 2, 0, 0, 0, 0, 0, 0, 0),
-    )
-    FRAME = (
-        (0, 1, 2, 0, 1, 2, 0, 1, 2, 0, 0, 1, 2, 0, 1, 2, 0, 1, 2, 0),
-        (0, 1, 0, 1, 2, 0, 1, 2, 2, 0, 0, 1, 0, 2, 1, 0, 1, 2, 2, 0),
-        (0, 1, 0, 1, 0, 1, 0, 0, 1, 0, 1, 0, 1, 0, 0, 0, 0, 0, 0, 0),
+    WORDS = (
+        (172066848, 379887846, 586692044, 658099826),
+        (174197792, 379887842, 521679278, 658099826),
+        (241306656, 551988553, 658099825, 658099827),
     )
     STEPS = 20
 
-    def choose(step, tables):
-        def at(table):
-            value = jnp.int32(table[-1])
-            for i in range(len(table) - 2, -1, -1):
-                value = jnp.where(step == i, table[i], value)
-            return value
-
-        return jnp.where(relay, at(tables[2]), jnp.where(bound, at(tables[1]), at(tables[0])))
+    kinds = (~(relay | bound), bound, relay)
+
+    def events_at(step):
+        for mine, events in zip(kinds, EVENTS):
+            if step in events:
+                @pl.when(mine)
+                def _():
+                    for entry in events[step]:
+                        entry[0](*entry[1:])
+
+    def dispatch(step, low, high):
+        if high - low == 1:
+            events_at(low)
+        elif high > low:
+            middle = (low + high) // 2
+
+            @pl.when(step < middle)
+            def _():
+                dispatch(step, low, middle)
+
+            @pl.when(step >= middle)
+            def _():
+                dispatch(step, middle, high)
+
+    def word(i):
+        return jnp.where(relay, WORDS[2][i], jnp.where(bound, WORDS[1][i], WORDS[0][i]))
 
     def queries_side(a, s, related):
         heads = range(HEADS)
@@ -303,26 +315,28 @@
             value_acc[n] += nn(weights.astype(jnp.bfloat16), out_grad)
             key_acc[n] += nn(inner, query)
 
-    def do_step(step, carry):
-        for mine, events in zip((~(relay | bound), bound, relay), EVENTS):
-            for at, entries in events.items():
-                @pl.when(mine & (step == at))
-                def _():
-                    for entry in entries:
-                        entry[0](*entry[1:])
-
-        kind, s, o = choose(step, KIND), choose(step, ROW), choose(step, FRAME)
+    def do_step(step, left_words):
+        dispatch(step, 0, STEPS)
+        now, later = left_words[0], left_words[1:]
+        digit = now % 32
+        kind = (digit >= 9).astype(jnp.int32) + (digit >= 10).astype(jnp.int32) + (digit >= 19).astype(jnp.int32)
+        tile = digit % 10
+        s, o = tile // 3, tile % 3
         a = jnp.where(o == 0, 1, jnp.where(o == 1, chip_here, off_here))
         there = ((s < 2) | z_from) & ((o < 2) | ~relay)
         related = ((t + a - 1) >= clip) == (t >= clip)
-        waits = (o > 0) & ~(bound & (o == 2) & (s == 1))
+        waits = (o == 2) & ~(bound & (s == 1))
 
         @pl.when(there & (kind == QUERIES))
         def _():
+            @pl.when(o == 1)
+            def _():
+                arrive_chip(s, 0)
+
             @pl.when(waits)
             def _():
                 for k in range(EARLY):
-                    arrive(a, s, k)
+                    arrive(s, k)
 
             queries_side(a, s, related)
 
@@ -332,10 +346,14 @@
 
         @pl.when(there & (kind == KEYS))
         def _():
+            @pl.when(o == 1)
+            def _():
+                arrive_chip(s, 1)
+
             @pl.when(waits)
             def _():
                 for k in range(EARLY, CHUNKS):
-                    arrive(a, s, k)
+                    arrive(s, k)
 
             @pl.when((s > 0) | (o > 0))
             def _():
@@ -343,40 +361,27 @@
 
             keys_side(a, s, related)
 
-        return carry
-
-    lax.fori_loop(0, STEPS, do_step, 0)
+        turn = step % 6 == 5
+        return tuple(
+            jnp.where(turn, after, before) for before, after in zip((now // 32,) + later, later + (jnp.int32(0),))
+        )
+
+    lax.fori_loop(0, STEPS, do_step, tuple(word(i) for i in range(len(WORDS[0]))))
 
     for n in range(HEADS):
         out_ref[2, :, columns(n)] = (key_acc[n] * scale).astype(jnp.bfloat16)
         out_ref[3, :, columns(n)] = value_acc[n].astype(jnp.bfloat16)
 
-    for k in range(CHUNKS):
-        to_chip(0, k).wait_send()
-        off_chip(0, k).wait_send()
-        to_chip(1, k).wait_send()
-
-        @pl.when(~relay)
-        def _():
-            off_chip(1, k).wait_send()
-
-        swap(k).wait_send()
-
-        @pl.when(z_to)
-        def _():
-            along_z(k).wait_send()
-
-        @pl.when(z_to & bound)
-        def _():
-            side_z(k).wait_send()
-
-        @pl.when(z_from)
-        def _():
-            to_chip(2, k).wait_send()
-
-        @pl.when(z_from & ~(relay | bound))
-        def _():
-            off_chip(2, k).wait_send()
+    def drain(place):
+        whole = tiles.at[1, 0]
+        remote(whole, whole, sent.at[place], sent.at[place], chip_dev).wait_send()
+
+    for place in (0, 3, 4, 6):
+        drain(place)
+    for place, used in ((1, z_to), (2, z_to & bound), (5, z_from), (7, ~relay), (8, z_from & ~(relay | bound))):
+        @pl.when(used)
+        def _():
+            drain(place)
 
     for dt, dh in neighbours:
         @pl.when(exists(dt, dh))
@@ -406,13 +411,11 @@
             pltpu.VMEM((HEADS, rows, dim), jnp.float32),
             pltpu.VMEM((HEADS, rows, dim), jnp.float32),
             pltpu.SemaphoreType.DMA((4,)),
+            pltpu.SemaphoreType.DMA((9,)),
             pltpu.SemaphoreType.DMA((CHUNKS,)),
             pltpu.SemaphoreType.DMA((CHUNKS,)),
-            pltpu.SemaphoreType.DMA((CHUNKS,)),
-            pltpu.SemaphoreType.DMA((CHUNKS,)),
-            pltpu.SemaphoreType.DMA((2, 3, CHUNKS)),
-            pltpu.SemaphoreType.DMA((3, 3, CHUNKS)),
-            pltpu.SemaphoreType.DMA((CHUNKS,)),
+            pltpu.SemaphoreType.DMA((3, 2)),
+            pltpu.SemaphoreType.DMA((3, CHUNKS)),
             pltpu.SemaphoreType.DMA((3, 3)),
             pltpu.SemaphoreType.DMA((3, 3)),
         ],

time: 52 us -> 47.1 us (0.906)
  Pallas kernels: 48.2 us -> 43.6 us
    pallas_call x1, Pallas kernels: 48.2 us -> 43.6 us  [shards(): pl.pallas_call(kernel, out_shape=jax.ShapeDtypeStruct((4, rows, channels)...]
where the time goes in v4:
time: 47.1 us; the launch traced here: 47 us
  Pallas kernels  43.6 us (93%)
  local copies, waits for them, and re-layouts  2.11 us (4%)
  between operations  1.29 us (3%)
    pallas_call x1, Pallas kernels, shards(): pl.pallas_call(kernel, out_shape=jax.ShapeDtypeStruct((4, rows, channels)...  43.6 us
    another operation x1, local copies, waits for them, and re-layouts, shards(): return tuple((outs[i].reshape(queries.shape) for i in range(4)))  2.11 us

profile of v4, /device:TPU:6, one launch (start us, length us, event | category | flops | bytes accessed | tf_op | source)
XLA Modules:
  0.0 47.0 jit_solution(10200041547218464200)
XLA Ops:
  1.3 43.6 %tile_attention.1 = bf16[4,384,256]{2,1,0:T(8,128)(2,1)} custom-call(s32[1]{0:T(128)S(6)} %copy.9.clip_ref, bf16[384,256]{1,0:T(8,128)(2,1)} %bitcast.12, bf16[384,256]{1,0:T(8,128)(2,1)} %bitcast.13, bf16[384,256]{1,0:T(8,128)(2,1)} %bitcast.14, bf16[384,256]{1,0:T(8,128)(2,1)} %bitcast.15), custom_call_target="tpu_custom_call" | custom-call | tf_op jit(solution)/shard_map/tile_attention/pallas_call | solution.py:397
  44.9 2.1 %slice_bitcast_fusion = (bf16[1,1,1,384,256]{4,3,2,1,0:T(8,128)(2,1)}, bf16[1,1,1,384,256]{4,3,2,1,0:T(8,128)(2,1)}, bf16[1,1,1,384,256]{4,3,2,1,0:T(8,128)(2,1)}, bf16[1,1,1,384,256]{4,3,2,1,0:T(8,128)(2,1)}) fusion(bf16[4,384,256]{2,1,0:T(8,128)(2,1)} %tile_attention.1), kind=kLoop, calls=%fused_computation | loop fusion | bytes 1572864 | tf_op jit(solution)/shard_map/reshape;squeeze | solution.py:427

commit v5 on v4

--- a/solution.py
+++ b/solution.py
@@ -11,7 +11,7 @@
 MESH = pl.DeviceIdType.MESH
 QUERIES, FINISH, KEYS, NOTHING = range(4)
 K, V, Q, G = range(4)
-PIECES = 2
+PIECES = 3
 EARLY = 2 * PIECES
 CHUNKS = 4 * PIECES
 
@@ -165,7 +165,7 @@
 
     for copy in copies:
         copy.wait()
-    for k in range(4):
+    for k in range(6):
         begin(k)
 
     clip = clip_ref[0]
@@ -182,48 +182,48 @@
 
     EVENTS = (
         {
-            2: [(on_swap, 0)],
-            3: [(on_swap, 1), (on_z, 0), (on_swap, 2), (on_swap, 3)],
-            4: [(on_z, 1), (begin, 4), (begin, 5)],
-            5: [(on_z, 2)],
-            6: [(on_z, 3)],
-            7: [(begin, 6), (begin, 7), (on_swap, 4)],
-            8: [(on_swap, 5)],
-            9: [(on_z, 4), (on_swap, 6)],
-            10: [(on_z, 5), (on_swap, 7)],
-            13: [(on_z, 6)],
-            14: [(on_z, 7)],
+            2: [(on_swap, 0), (on_swap, 1)],
+            3: [(on_swap, 2), (on_z, 0), (on_swap, 3), (on_z, 1), (on_swap, 4), (begin, 6), (begin, 7), (begin, 8), (on_z, 2), (on_swap, 5)],
+            4: [(on_z, 3)],
+            5: [(on_z, 4), (on_swap, 6), (on_z, 5)],
+            6: [(begin, 9), (begin, 10), (begin, 11), (on_swap, 7), (on_swap, 8), (on_z, 6)],
+            8: [(on_z, 7), (on_swap, 9), (on_z, 8), (on_swap, 10)],
+            9: [(on_swap, 11)],
+            10: [(on_z, 9)],
+            11: [(on_z, 10), (on_z, 11)],
         },
         {
-            2: [(on_swap, 0), (on_swap, 1), (on_z, 0), (on_swap, 2), (on_z, 1), (on_swap, 3)],
-            3: [(on_z, 2), (begin, 4), (begin, 5), (on_side, 0)],
-            4: [(on_side, 1), (on_z, 3), (on_side, 2)],
+            2: [(on_swap, 0), (on_swap, 1), (on_swap, 2), (on_z, 0), (on_swap, 3), (on_z, 1), (on_swap, 4), (on_z, 2), (on_swap, 5)],
+            3: [(on_z, 3), (on_side, 0), (on_side, 1)],
+            4: [(on_z, 4), (begin, 6), (begin, 7), (begin, 8), (on_side, 2), (on_z, 5)],
             5: [(on_side, 3)],
-            6: [(begin, 6), (begin, 7)],
-            7: [(on_swap, 4)],
-            8: [(on_swap, 5)],
-            10: [(on_swap, 6), (on_z, 4)],
-            11: [(on_z, 5), (on_swap, 7)],
-            12: [(on_side, 4), (on_side, 5)],
-            14: [(on_side, 6), (on_z, 6)],
-            15: [(on_z, 7), (on_side, 7)],
+            6: [(on_side, 4), (begin, 9), (begin, 10), (begin, 11), (on_side, 5), (on_swap, 6)],
+            7: [(on_swap, 7)],
+            8: [(on_swap, 8)],
+            9: [(on_swap, 9), (on_z, 6)],
+            10: [(on_swap, 10), (on_z, 7), (on_swap, 11), (on_side, 6)],
+            11: [(on_z, 8), (on_side, 7), (on_side, 8)],
+            12: [(on_z, 9), (on_side, 9)],
+            13: [(on_z, 10)],
+            14: [(on_z, 11), (on_side, 10)],
+            15: [(on_side, 11)],
         },
         {
-            2: [(on_relay, 0), (on_relay, 1), (on_swap, 0), (on_relay, 2), (on_relay, 3), (on_swap, 1), (on_z, 0), (on_swap, 2), (on_z, 1), (on_swap, 3), (begin, 4), (begin, 5)],
-            4: [(on_z, 2), (on_relay, 4), (on_z, 3)],
-            5: [(begin, 6), (begin, 7), (on_relay, 5)],
-            6: [(on_swap, 4)],
-            7: [(on_swap, 5)],
-            8: [(on_relay, 6), (on_relay, 7), (on_z, 4), (on_z, 5), (on_swap, 6)],
-            9: [(on_swap, 7)],
-            10: [(on_z, 6)],
-            11: [(on_z, 7)],
+            2: [(on_relay, 0), (on_relay, 1), (on_swap, 0), (on_relay, 2), (on_relay, 3), (on_swap, 1), (on_relay, 4), (on_relay, 5), (on_swap, 2), (on_z, 0), (on_swap, 3), (on_z, 1), (on_z, 2), (on_swap, 4), (begin, 6), (begin, 7), (begin, 8), (on_swap, 5)],
+            3: [(on_z, 3)],
+            4: [(on_z, 4), (on_z, 5)],
+            5: [(begin, 9), (begin, 10), (begin, 11)],
+            6: [(on_relay, 6), (on_relay, 7)],
+            7: [(on_swap, 6), (on_relay, 8), (on_swap, 7)],
+            8: [(on_relay, 9), (on_swap, 8), (on_z, 6), (on_relay, 10), (on_relay, 11), (on_swap, 9), (on_z, 7), (on_swap, 10), (on_swap, 11), (on_z, 8)],
+            9: [(on_z, 9)],
+            10: [(on_z, 10), (on_z, 11)],
         },
     )
     WORDS = (
-        (172066848, 379887846, 586692044, 658099826),
-        (174197792, 379887842, 521679278, 658099826),
-        (241306656, 551988553, 658099825, 658099827),
+        (205621280, 379887783, 587611597, 658099826),
+        (241306656, 379887778, 587706798, 658099826),
+        (241306656, 486976841, 658099825, 658099827),
     )
     STEPS = 20
 
@@ -392,11 +392,14 @@
 def shards(queries, key_states, value_states, out_grad, clip_start):
     rows, channels = queries.shape[-2:]
     dim = channels // HEADS
-    flat = [x.reshape(rows, channels) for x in (queries, key_states, value_states, out_grad)]
+    flat = [
+        pltpu.with_memory_space_constraint(x.reshape(rows, channels), pltpu.HBM)
+        for x in (queries, key_states, value_states, out_grad)
+    ]
     vmem = pl.BlockSpec(memory_space=pltpu.VMEM)
     outs = pl.pallas_call(
         kernel,
-        out_shape=jax.ShapeDtypeStruct((4, rows, channels), jnp.bfloat16),
+        out_shape=pltpu.VMEM((4, rows, channels), jnp.bfloat16),
         in_specs=[pl.BlockSpec(memory_space=pltpu.SMEM)] + [pl.BlockSpec(memory_space=pltpu.HBM)] * 4,
         out_specs=vmem,
         scratch_shapes=[
@@ -420,7 +423,7 @@
             pltpu.SemaphoreType.DMA((3, 3)),
         ],
         compiler_params=pltpu.CompilerParams(
-            collective_id=0, has_side_effects=True, vmem_limit_bytes=64 * 2**20
+            collective_id=0, has_side_effects=True, vmem_limit_bytes=48 * 2**20
         ),
         name="tile_attention",
     )(clip_start, *flat)

time: 47.1 us -> 43.9 us (0.932)
  Pallas kernels: 43.6 us -> 41.6 us
  local copies, waits for them, and re-layouts: 2.11 us -> 0.89 us
    pallas_call x1, Pallas kernels: 43.6 us -> 41.6 us  [shards(): pl.pallas_call(kernel, out_shape=pltpu.VMEM((4, rows, channels), jnp.bflo...]
    another operation x1, local copies, waits for them, and re-layouts: 2.11 us -> 0.89 us  [shards(): return tuple((outs[i].reshape(queries.shape) for i in range(4)))]
where the time goes in v5:
time: 43.9 us; the launch traced here: 43.8 us
  Pallas kernels  41.6 us (95%)
  between operations  1.29 us (3%)
  local copies, waits for them, and re-layouts  0.89 us (2%)
    pallas_call x1, Pallas kernels, shards(): pl.pallas_call(kernel, out_shape=pltpu.VMEM((4, rows, channels), jnp.bflo...  41.6 us
    another operation x1, local copies, waits for them, and re-layouts, shards(): return tuple((outs[i].reshape(queries.shape) for i in range(4)))  0.89 us

profile of v5, /device:TPU:6, one launch (start us, length us, event | category | flops | bytes accessed | tf_op | source)
XLA Modules:
  0.0 43.8 jit_solution(529850099976855677)
XLA Ops:
  1.3 41.6 %tile_attention.1 = bf16[4,384,256]{2,1,0:T(8,128)(2,1)S(1)} custom-call(s32[1]{0:T(128)S(6)} %copy.9.clip_ref, bf16[384,256]{1,0:T(8,128)(2,1)} %bitcast.12, bf16[384,256]{1,0:T(8,128)(2,1)} %bitcast.13, bf16[384,256]{1,0:T(8,128)(2,1)} %bitcast.14, bf16[384,256]{1,0:T(8,128)(2,1)} %bitcast.15), custom_call_target="tpu_custom_call" | custom-call | tf_op jit(solution)/shard_map/tile_attention/pallas_call | solution.py:400
  42.9 0.9 %slice_bitcast_fusion = (bf16[1,1,1,384,256]{4,3,2,1,0:T(8,128)(2,1)}, bf16[1,1,1,384,256]{4,3,2,1,0:T(8,128)(2,1)}, bf16[1,1,1,384,256]{4,3,2,1,0:T(8,128)(2,1)}, bf16[1,1,1,384,256]{4,3,2,1,0:T(8,128)(2,1)}) fusion(bf16[4,384,256]{2,1,0:T(8,128)(2,1)S(1)} %tile_attention.1), kind=kLoop, calls=%fused_computation | loop fusion | bytes 1572864 | tf_op jit(solution)/shard_map/reshape;squeeze | solution.py:430

commit v6 on v5

--- a/solution.py
+++ b/solution.py
@@ -9,11 +9,12 @@
 LOG2E = 1.4426950408889634
 NEGATIVE = -1e30
 MESH = pl.DeviceIdType.MESH
-QUERIES, FINISH, KEYS, NOTHING = range(4)
+FINISH, KEYS, PAIRS, NOTHING = 9, 10, 19, 22
 K, V, Q, G = range(4)
 PIECES = 3
 EARLY = 2 * PIECES
 CHUNKS = 4 * PIECES
+DIRECT = (9, 10, 11,)
 
 
 def nt(left, right):
@@ -127,7 +128,7 @@
         return remote(stats.at[1, 0], stats.at[a, s], stats_send.at[a, dh + 1], stats_recv.at[a, s], (t + dt, h + dh))
 
     def spread(s, k):
-        @pl.when(~(relay | bound) if s == 2 else ~relay)
+        @pl.when(~(relay | bound) if s == 2 and k not in DIRECT else ~relay)
         def _():
             off_chip(s, k).start()
 
@@ -135,7 +136,10 @@
 
     def begin(k):
         swap(k).start()
-        spread(0, k)
+
+        @pl.when(~relay)
+        def _():
+            off_chip(0, k).start()
 
     def on_swap(k):
         swap(k).wait_recv()
@@ -165,8 +169,10 @@
 
     for copy in copies:
         copy.wait()
-    for k in range(6):
-        begin(k)
+    for k in range(CHUNKS):
+        if k in range(6):
+            begin(k)
+        to_chip(0, k).start()
 
     clip = clip_ref[0]
 
@@ -183,49 +189,47 @@
     EVENTS = (
         {
             2: [(on_swap, 0), (on_swap, 1)],
-            3: [(on_swap, 2), (on_z, 0), (on_swap, 3), (on_z, 1), (on_swap, 4), (begin, 6), (begin, 7), (begin, 8), (on_z, 2), (on_swap, 5)],
+            3: [(on_swap, 2), (on_z, 0), (on_swap, 3), (on_z, 1), (on_swap, 4), (on_swap, 5), (on_z, 2), (begin, 6), (begin, 7), (begin, 8)],
             4: [(on_z, 3)],
-            5: [(on_z, 4), (on_swap, 6), (on_z, 5)],
-            6: [(begin, 9), (begin, 10), (begin, 11), (on_swap, 7), (on_swap, 8), (on_z, 6)],
-            8: [(on_z, 7), (on_swap, 9), (on_z, 8), (on_swap, 10)],
-            9: [(on_swap, 11)],
-            10: [(on_z, 9)],
-            11: [(on_z, 10), (on_z, 11)],
+            5: [(on_z, 4), (on_swap, 6)],
+            6: [(on_z, 5), (on_swap, 7), (begin, 9), (begin, 10), (begin, 11)],
+            7: [(on_swap, 8), (on_z, 6)],
+            8: [(on_z, 7), (on_swap, 9)],
+            9: [(on_swap, 10)],
+            10: [(on_z, 8), (on_swap, 11), (on_z, 9)],
+            11: [(on_z, 10)],
+            13: [(on_z, 11)],
         },
         {
             2: [(on_swap, 0), (on_swap, 1), (on_swap, 2), (on_z, 0), (on_swap, 3), (on_z, 1), (on_swap, 4), (on_z, 2), (on_swap, 5)],
-            3: [(on_z, 3), (on_side, 0), (on_side, 1)],
-            4: [(on_z, 4), (begin, 6), (begin, 7), (begin, 8), (on_side, 2), (on_z, 5)],
-            5: [(on_side, 3)],
-            6: [(on_side, 4), (begin, 9), (begin, 10), (begin, 11), (on_side, 5), (on_swap, 6)],
-            7: [(on_swap, 7)],
+            3: [(on_side, 0), (on_z, 3), (on_side, 1)],
+            4: [(begin, 6), (begin, 7), (begin, 8), (on_side, 2), (on_z, 4), (on_side, 3), (on_z, 5)],
+            5: [(on_side, 4)],
+            6: [(on_side, 5), (begin, 9), (begin, 10), (begin, 11)],
+            7: [(on_swap, 6), (on_swap, 7)],
             8: [(on_swap, 8)],
-            9: [(on_swap, 9), (on_z, 6)],
-            10: [(on_swap, 10), (on_z, 7), (on_swap, 11), (on_side, 6)],
-            11: [(on_z, 8), (on_side, 7), (on_side, 8)],
-            12: [(on_z, 9), (on_side, 9)],
-            13: [(on_z, 10)],
-            14: [(on_z, 11), (on_side, 10)],
-            15: [(on_side, 11)],
+            9: [(on_swap, 9)],
+            10: [(on_z, 6), (on_swap, 10), (on_z, 7), (on_swap, 11), (on_z, 8)],
+            11: [(on_side, 6), (on_z, 9), (on_side, 7), (on_side, 8), (on_z, 10)],
+            12: [(on_z, 11)],
         },
         {
-            2: [(on_relay, 0), (on_relay, 1), (on_swap, 0), (on_relay, 2), (on_relay, 3), (on_swap, 1), (on_relay, 4), (on_relay, 5), (on_swap, 2), (on_z, 0), (on_swap, 3), (on_z, 1), (on_z, 2), (on_swap, 4), (begin, 6), (begin, 7), (begin, 8), (on_swap, 5)],
-            3: [(on_z, 3)],
+            2: [(on_relay, 0), (on_relay, 1), (on_swap, 0), (on_relay, 2), (on_relay, 3), (on_swap, 1), (on_relay, 4), (on_relay, 5), (on_swap, 2), (on_z, 0), (on_swap, 3), (on_z, 1), (on_swap, 4), (on_z, 2), (on_swap, 5)],
+            3: [(begin, 6), (begin, 7), (begin, 8), (on_z, 3)],
             4: [(on_z, 4), (on_z, 5)],
-            5: [(begin, 9), (begin, 10), (begin, 11)],
-            6: [(on_relay, 6), (on_relay, 7)],
-            7: [(on_swap, 6), (on_relay, 8), (on_swap, 7)],
-            8: [(on_relay, 9), (on_swap, 8), (on_z, 6), (on_relay, 10), (on_relay, 11), (on_swap, 9), (on_z, 7), (on_swap, 10), (on_swap, 11), (on_z, 8)],
-            9: [(on_z, 9)],
-            10: [(on_z, 10), (on_z, 11)],
+            5: [(begin, 9), (begin, 10), (begin, 11), (on_relay, 6)],
+            6: [(on_relay, 7), (on_relay, 8), (on_swap, 6), (on_swap, 7)],
+            7: [(on_swap, 8), (on_relay, 9), (on_swap, 9), (on_relay, 10), (on_relay, 11), (on_z, 6), (on_swap, 10)],
+            8: [(on_z, 7), (on_swap, 11), (on_z, 8), (on_z, 9), (on_z, 10)],
+            9: [(on_z, 11)],
         },
     )
     WORDS = (
-        (205621280, 379887783, 587611597, 658099826),
-        (241306656, 379887778, 587706798, 658099826),
-        (241306656, 486976841, 658099825, 658099827),
+        (172066848, 422879462, 761878004),
+        (73534496, 691314855, 761877996),
+        (241306656, 761975401, 762010326),
     )
-    STEPS = 20
+    STEPS = 17
 
     kinds = (~(relay | bound), bound, relay)
 
@@ -304,62 +308,88 @@
             own_grad = (grad[n] - (dot - row_dot[n]) * sums[dim:]) * (scale / total)
             out_ref[1, :, columns(n)] = own_grad.T.astype(jnp.bfloat16)
 
-    def keys_side(a, s, related):
+    def keys_side(s, frames):
         for n in range(HEADS):
             own_k, own_v = tiles[1, 0, K, :, columns(n)], tiles[1, 0, V, :, columns(n)]
-            query, out_grad = tiles[a, s, Q, :, columns(n)], tiles[a, s, G, :, columns(n)]
-            log_total = jnp.where(related, stats[a, s, n : n + 1], -NEGATIVE)
-            dot = stats[a, s, HEADS + n : HEADS + n + 1]
-            weights = jnp.exp2(nt(own_k, query) * to_log2 - log_total)
-            inner = (weights * (nt(own_v, out_grad) - dot)).astype(jnp.bfloat16)
-            value_acc[n] += nn(weights.astype(jnp.bfloat16), out_grad)
-            key_acc[n] += nn(inner, query)
+            to_value, to_key = [], []
+            for a, counts in frames:
+                query, out_grad = tiles[a, s, Q, :, columns(n)], tiles[a, s, G, :, columns(n)]
+                log_total = jnp.where(counts, stats[a, s, n : n + 1], -NEGATIVE)
+                dot = stats[a, s, HEADS + n : HEADS + n + 1]
+                weights = jnp.exp2(nt(own_k, query) * to_log2 - log_total)
+                inner = (weights * (nt(own_v, out_grad) - dot)).astype(jnp.bfloat16)
+                to_value.append(nn(weights.astype(jnp.bfloat16), out_grad))
+                to_key.append(nn(inner, query))
+            value_acc[n] += sum(to_value[1:], to_value[0])
+            key_acc[n] += sum(to_key[1:], to_key[0])
+
+    def frame(o):
+        a = jnp.where(o == 0, 1, jnp.where(o == 1, chip_here, off_here))
+        return a, ((t + a - 1) >= clip) == (t >= clip)
+
+    def arrive_stats(a, s):
+        remote(stats.at[1, 0], stats.at[a, s], stats_send.at[1, 1], stats_recv.at[a, s], chip_dev).wait_recv()
 
     def do_step(step, left_words):
         dispatch(step, 0, STEPS)
         now, later = left_words[0], left_words[1:]
         digit = now % 32
-        kind = (digit >= 9).astype(jnp.int32) + (digit >= 10).astype(jnp.int32) + (digit >= 19).astype(jnp.int32)
-        tile = digit % 10
-        s, o = tile // 3, tile % 3
-        a = jnp.where(o == 0, 1, jnp.where(o == 1, chip_here, off_here))
-        there = ((s < 2) | z_from) & ((o < 2) | ~relay)
-        related = ((t + a - 1) >= clip) == (t >= clip)
-        waits = (o == 2) & ~(bound & (s == 1))
-
-        @pl.when(there & (kind == QUERIES))
+        s, o = digit // 3, digit % 3
+
+        @pl.when((digit < 9) & ((s < 2) | z_from) & ((o < 2) | ~relay))
         def _():
             @pl.when(o == 1)
             def _():
                 arrive_chip(s, 0)
 
-            @pl.when(waits)
+            @pl.when((o == 2) & ~(bound & (s == 1)))
             def _():
                 for k in range(EARLY):
                     arrive(s, k)
 
-            queries_side(a, s, related)
-
-        @pl.when(kind == FINISH)
+            queries_side(frame(o)[0], s, frame(o)[1])
+
+        @pl.when(digit == FINISH)
         def _():
             finish_queries()
 
-        @pl.when(there & (kind == KEYS))
+        single = digit - KEYS
+        row, o = single // 3, single % 3
+
+        @pl.when((digit >= KEYS) & (digit < PAIRS) & ((row < 2) | z_from) & ((o < 2) | ~relay))
         def _():
             @pl.when(o == 1)
             def _():
-                arrive_chip(s, 1)
-
-            @pl.when(waits)
+                arrive_chip(row, 1)
+
+            @pl.when(o == 2)
             def _():
                 for k in range(EARLY, CHUNKS):
-                    arrive(s, k)
-
-            @pl.when((s > 0) | (o > 0))
-            def _():
-                remote(stats.at[1, 0], stats.at[a, s], stats_send.at[1, 1], stats_recv.at[a, s], chip_dev).wait_recv()
-
-            keys_side(a, s, related)
+                    if k in DIRECT:
+                        arrive(row, k)
+                    else:
+                        @pl.when(~(bound & (row == 1)))
+                        def _():
+                            arrive(row, k)
+
+            @pl.when(single > 0)
+            def _():
+                arrive_stats(frame(o)[0], row)
+
+            keys_side(row, (frame(o),))
+
+        pair = digit - PAIRS
+
+        @pl.when((digit >= PAIRS) & (digit < NOTHING) & ((pair < 2) | z_from))
+        def _():
+            arrive_chip(pair, 1)
+            arrive_stats(chip_here, pair)
+
+            @pl.when(pair > 0)
+            def _():
+                arrive_stats(1, pair)
+
+            keys_side(pair, (frame(0), frame(1)))
 
         turn = step % 6 == 5
         return tuple(
@@ -372,16 +402,21 @@
         out_ref[2, :, columns(n)] = (key_acc[n] * scale).astype(jnp.bfloat16)
         out_ref[3, :, columns(n)] = value_acc[n].astype(jnp.bfloat16)
 
-    def drain(place):
-        whole = tiles.at[1, 0]
+    def drain(place, arrays=4):
+        whole = tiles.at[1, 0, pl.ds(0, arrays)]
         remote(whole, whole, sent.at[place], sent.at[place], chip_dev).wait_send()
 
+    direct = len(DIRECT) // PIECES
+    usual = ~(relay | bound)
     for place in (0, 3, 4, 6):
         drain(place)
-    for place, used in ((1, z_to), (2, z_to & bound), (5, z_from), (7, ~relay), (8, z_from & ~(relay | bound))):
-        @pl.when(used)
-        def _():
-            drain(place)
+    for place, used, arrays in (
+        (1, z_to, 4), (2, z_to & bound, 4 - direct), (5, z_from, 4), (7, ~relay, 4), (8, z_from & usual, 4), (8, z_from & bound, direct)
+    ):
+        if arrays:
+            @pl.when(used)
+            def _():
+                drain(place, arrays)
 
     for dt, dh in neighbours:
         @pl.when(exists(dt, dh))

time: 43.9 us -> 43.2 us (0.984)
  Pallas kernels: 41.6 us -> 40.9 us
    pallas_call x1, Pallas kernels: 41.6 us -> 40.9 us  [shards(): pl.pallas_call(kernel, out_shape=pltpu.VMEM((4, rows, channels), jnp.bflo...]
where the time goes in v6:
time: 43.2 us; the launch traced here: 43 us
  Pallas kernels  40.9 us (95%)
  between operations  1.29 us (3%)
  local copies, waits for them, and re-layouts  0.89 us (2%)
    pallas_call x1, Pallas kernels, shards(): pl.pallas_call(kernel, out_shape=pltpu.VMEM((4, rows, channels), jnp.bflo...  40.9 us
    another operation x1, local copies, waits for them, and re-layouts, shards(): return tuple((outs[i].reshape(queries.shape) for i in range(4)))  0.89 us

profile of v6, /device:TPU:6, one launch (start us, length us, event | category | flops | bytes accessed | tf_op | source)
XLA Modules:
  0.0 43.0 jit_solution(3326487339611936284)
XLA Ops:
  1.3 40.9 %tile_attention.1 = bf16[4,384,256]{2,1,0:T(8,128)(2,1)S(1)} custom-call(s32[1]{0:T(128)S(6)} %copy.9.clip_ref, bf16[384,256]{1,0:T(8,128)(2,1)} %bitcast.12, bf16[384,256]{1,0:T(8,128)(2,1)} %bitcast.13, bf16[384,256]{1,0:T(8,128)(2,1)} %bitcast.14, bf16[384,256]{1,0:T(8,128)(2,1)} %bitcast.15), custom_call_target="tpu_custom_call" | custom-call | tf_op jit(solution)/shard_map/tile_attention/pallas_call | solution.py:435
  42.2 0.9 %slice_bitcast_fusion = (bf16[1,1,1,384,256]{4,3,2,1,0:T(8,128)(2,1)}, bf16[1,1,1,384,256]{4,3,2,1,0:T(8,128)(2,1)}, bf16[1,1,1,384,256]{4,3,2,1,0:T(8,128)(2,1)}, bf16[1,1,1,384,256]{4,3,2,1,0:T(8,128)(2,1)}) fusion(bf16[4,384,256]{2,1,0:T(8,128)(2,1)S(1)} %tile_attention.1), kind=kLoop, calls=%fused_computation | loop fusion | bytes 1572864 | tf_op jit(solution)/shard_map/reshape;squeeze | solution.py:465

commit v7 on v6

--- a/solution.py
+++ b/solution.py
@@ -188,44 +188,46 @@
 
     EVENTS = (
         {
-            2: [(on_swap, 0), (on_swap, 1)],
-            3: [(on_swap, 2), (on_z, 0), (on_swap, 3), (on_z, 1), (on_swap, 4), (on_swap, 5), (on_z, 2), (begin, 6), (begin, 7), (begin, 8)],
+            0: [(on_swap, 0)],
+            1: [(on_swap, 1)],
+            2: [(on_swap, 2), (on_z, 0), (on_swap, 3)],
+            3: [(on_swap, 4), (on_z, 1), (on_swap, 5), (begin, 6), (begin, 7), (on_z, 2), (begin, 8)],
             4: [(on_z, 3)],
             5: [(on_z, 4), (on_swap, 6)],
             6: [(on_z, 5), (on_swap, 7), (begin, 9), (begin, 10), (begin, 11)],
             7: [(on_swap, 8), (on_z, 6)],
             8: [(on_z, 7), (on_swap, 9)],
             9: [(on_swap, 10)],
-            10: [(on_z, 8), (on_swap, 11), (on_z, 9)],
-            11: [(on_z, 10)],
-            13: [(on_z, 11)],
+            10: [(on_swap, 11), (on_z, 8)],
+            11: [(on_z, 9), (on_z, 10)],
+            12: [(on_z, 11)],
         },
         {
-            2: [(on_swap, 0), (on_swap, 1), (on_swap, 2), (on_z, 0), (on_swap, 3), (on_z, 1), (on_swap, 4), (on_z, 2), (on_swap, 5)],
-            3: [(on_side, 0), (on_z, 3), (on_side, 1)],
+            2: [(on_swap, 0), (on_swap, 1), (on_swap, 2), (on_z, 0), (on_swap, 3), (on_z, 1), (on_swap, 4), (on_swap, 5)],
+            3: [(on_z, 2), (on_side, 0), (on_z, 3), (on_side, 1)],
             4: [(begin, 6), (begin, 7), (begin, 8), (on_side, 2), (on_z, 4), (on_side, 3), (on_z, 5)],
             5: [(on_side, 4)],
-            6: [(on_side, 5), (begin, 9), (begin, 10), (begin, 11)],
-            7: [(on_swap, 6), (on_swap, 7)],
+            6: [(on_side, 5), (begin, 9), (begin, 10), (on_swap, 6), (begin, 11)],
+            7: [(on_swap, 7)],
             8: [(on_swap, 8)],
-            9: [(on_swap, 9)],
-            10: [(on_z, 6), (on_swap, 10), (on_z, 7), (on_swap, 11), (on_z, 8)],
+            9: [(on_swap, 9), (on_z, 6)],
+            10: [(on_swap, 10), (on_z, 7), (on_swap, 11), (on_z, 8)],
             11: [(on_side, 6), (on_z, 9), (on_side, 7), (on_side, 8), (on_z, 10)],
             12: [(on_z, 11)],
         },
         {
-            2: [(on_relay, 0), (on_relay, 1), (on_swap, 0), (on_relay, 2), (on_relay, 3), (on_swap, 1), (on_relay, 4), (on_relay, 5), (on_swap, 2), (on_z, 0), (on_swap, 3), (on_z, 1), (on_swap, 4), (on_z, 2), (on_swap, 5)],
-            3: [(begin, 6), (begin, 7), (begin, 8), (on_z, 3)],
-            4: [(on_z, 4), (on_z, 5)],
-            5: [(begin, 9), (begin, 10), (begin, 11), (on_relay, 6)],
-            6: [(on_relay, 7), (on_relay, 8), (on_swap, 6), (on_swap, 7)],
-            7: [(on_swap, 8), (on_relay, 9), (on_swap, 9), (on_relay, 10), (on_relay, 11), (on_z, 6), (on_swap, 10)],
+            2: [(on_relay, 0), (on_relay, 1), (on_swap, 0), (on_relay, 2), (on_relay, 3), (on_swap, 1), (on_relay, 4), (on_relay, 5), (on_swap, 2), (on_z, 0), (on_swap, 3), (on_z, 1), (on_swap, 4), (on_swap, 5), (on_z, 2)],
+            3: [(begin, 6), (begin, 7), (on_z, 3), (on_z, 4), (on_z, 5)],
+            4: [(begin, 8)],
+            5: [(begin, 9), (begin, 10), (begin, 11), (on_relay, 6), (on_relay, 7), (on_relay, 8), (on_swap, 6)],
+            6: [(on_swap, 7), (on_swap, 8)],
+            7: [(on_relay, 9), (on_swap, 9), (on_relay, 10), (on_relay, 11), (on_z, 6), (on_swap, 10)],
             8: [(on_z, 7), (on_swap, 11), (on_z, 8), (on_z, 9), (on_z, 10)],
             9: [(on_z, 11)],
         },
     )
     WORDS = (
-        (172066848, 422879462, 761878004),
+        (172065856, 422879462, 761878004),
         (73534496, 691314855, 761877996),
         (241306656, 761975401, 762010326),
     )

time: 43.2 us -> 42.6 us (0.986)
  Pallas kernels: 40.9 us -> 40.4 us
    pallas_call x1, Pallas kernels: 40.9 us -> 40.4 us  [shards(): pl.pallas_call(kernel, out_shape=pltpu.VMEM((4, rows, channels), jnp.bflo...]
where the time goes in v7:
time: 42.6 us; the launch traced here: 42.5 us
  Pallas kernels  40.4 us (95%)
  between operations  1.29 us (3%)
  local copies, waits for them, and re-layouts  0.89 us (2%)
    pallas_call x1, Pallas kernels, shards(): pl.pallas_call(kernel, out_shape=pltpu.VMEM((4, rows, channels), jnp.bflo...  40.4 us
    another operation x1, local copies, waits for them, and re-layouts, shards(): return tuple((outs[i].reshape(queries.shape) for i in range(4)))  0.89 us

profile of v7, /device:TPU:6, one launch (start us, length us, event | category | flops | bytes accessed | tf_op | source)
XLA Modules:
  0.0 42.5 jit_solution(15499901085566790532)
XLA Ops:
  1.3 40.4 %tile_attention.1 = bf16[4,384,256]{2,1,0:T(8,128)(2,1)S(1)} custom-call(s32[1]{0:T(128)S(6)} %copy.9.clip_ref, bf16[384,256]{1,0:T(8,128)(2,1)} %bitcast.12, bf16[384,256]{1,0:T(8,128)(2,1)} %bitcast.13, bf16[384,256]{1,0:T(8,128)(2,1)} %bitcast.14, bf16[384,256]{1,0:T(8,128)(2,1)} %bitcast.15), custom_call_target="tpu_custom_call" | custom-call | tf_op jit(solution)/shard_map/tile_attention/pallas_call | solution.py:437
  41.6 0.9 %slice_bitcast_fusion = (bf16[1,1,1,384,256]{4,3,2,1,0:T(8,128)(2,1)}, bf16[1,1,1,384,256]{4,3,2,1,0:T(8,128)(2,1)}, bf16[1,1,1,384,256]{4,3,2,1,0:T(8,128)(2,1)}, bf16[1,1,1,384,256]{4,3,2,1,0:T(8,128)(2,1)}) fusion(bf16[4,384,256]{2,1,0:T(8,128)(2,1)S(1)} %tile_attention.1), kind=kLoop, calls=%fused_computation | loop fusion | bytes 1572864 | tf_op jit(solution)/shard_map/reshape;squeeze | solution.py:467

commit v8 on v6

--- a/solution.py
+++ b/solution.py
@@ -198,27 +198,28 @@
             9: [(on_swap, 10)],
             10: [(on_z, 8), (on_swap, 11), (on_z, 9)],
             11: [(on_z, 10)],
-            13: [(on_z, 11)],
+            12: [(on_z, 11)],
         },
         {
-            2: [(on_swap, 0), (on_swap, 1), (on_swap, 2), (on_z, 0), (on_swap, 3), (on_z, 1), (on_swap, 4), (on_z, 2), (on_swap, 5)],
-            3: [(on_side, 0), (on_z, 3), (on_side, 1)],
-            4: [(begin, 6), (begin, 7), (begin, 8), (on_side, 2), (on_z, 4), (on_side, 3), (on_z, 5)],
+            1: [(on_swap, 0), (on_swap, 1), (on_swap, 2)],
+            2: [(on_z, 0), (on_swap, 3), (on_z, 1), (on_swap, 4), (on_swap, 5)],
+            3: [(on_z, 2), (on_side, 0), (on_z, 3), (on_side, 1)],
+            4: [(begin, 6), (begin, 7), (on_side, 2), (on_side, 3), (begin, 8), (on_z, 4), (on_z, 5)],
             5: [(on_side, 4)],
-            6: [(on_side, 5), (begin, 9), (begin, 10), (begin, 11)],
-            7: [(on_swap, 6), (on_swap, 7)],
+            6: [(on_side, 5), (begin, 9), (begin, 10), (on_swap, 6), (begin, 11)],
+            7: [(on_swap, 7)],
             8: [(on_swap, 8)],
-            9: [(on_swap, 9)],
-            10: [(on_z, 6), (on_swap, 10), (on_z, 7), (on_swap, 11), (on_z, 8)],
+            9: [(on_swap, 9), (on_z, 6)],
+            10: [(on_swap, 10), (on_z, 7), (on_z, 8), (on_swap, 11)],
             11: [(on_side, 6), (on_z, 9), (on_side, 7), (on_side, 8), (on_z, 10)],
             12: [(on_z, 11)],
         },
         {
-            2: [(on_relay, 0), (on_relay, 1), (on_swap, 0), (on_relay, 2), (on_relay, 3), (on_swap, 1), (on_relay, 4), (on_relay, 5), (on_swap, 2), (on_z, 0), (on_swap, 3), (on_z, 1), (on_swap, 4), (on_z, 2), (on_swap, 5)],
-            3: [(begin, 6), (begin, 7), (begin, 8), (on_z, 3)],
+            2: [(on_relay, 0), (on_relay, 1), (on_swap, 0), (on_relay, 2), (on_relay, 3), (on_swap, 1), (on_relay, 4), (on_relay, 5), (on_swap, 2), (on_z, 0), (on_swap, 3), (on_z, 1), (on_z, 2), (on_swap, 4), (on_swap, 5)],
+            3: [(begin, 6), (begin, 7), (on_z, 3), (begin, 8)],
             4: [(on_z, 4), (on_z, 5)],
-            5: [(begin, 9), (begin, 10), (begin, 11), (on_relay, 6)],
-            6: [(on_relay, 7), (on_relay, 8), (on_swap, 6), (on_swap, 7)],
+            5: [(begin, 9), (begin, 10), (begin, 11), (on_relay, 6), (on_relay, 7), (on_relay, 8), (on_swap, 6)],
+            6: [(on_swap, 7)],
             7: [(on_swap, 8), (on_relay, 9), (on_swap, 9), (on_relay, 10), (on_relay, 11), (on_z, 6), (on_swap, 10)],
             8: [(on_z, 7), (on_swap, 11), (on_z, 8), (on_z, 9), (on_z, 10)],
             9: [(on_z, 11)],
@@ -226,7 +227,7 @@
     )
     WORDS = (
         (172066848, 422879462, 761878004),
-        (73534496, 691314855, 761877996),
+        (73534496, 691314855, 761872044),
         (241306656, 761975401, 762010326),
     )
     STEPS = 17

time: 43.2 us -> 42.4 us (0.981)
  Pallas kernels: 40.9 us -> 40.1 us
    pallas_call x1, Pallas kernels: 40.9 us -> 40.1 us  [shards(): pl.pallas_call(kernel, out_shape=pltpu.VMEM((4, rows, channels), jnp.bflo...]
where the time goes in v8:
time: 42.4 us; the launch traced here: 42.3 us
  Pallas kernels  40.1 us (95%)
  between operations  1.29 us (3%)
  local copies, waits for them, and re-layouts  0.89 us (2%)
    pallas_call x1, Pallas kernels, shards(): pl.pallas_call(kernel, out_shape=pltpu.VMEM((4, rows, channels), jnp.bflo...  40.1 us
    another operation x1, local copies, waits for them, and re-layouts, shards(): return tuple((outs[i].reshape(queries.shape) for i in range(4)))  0.89 us

profile of v8, /device:TPU:6, one launch (start us, length us, event | category | flops | bytes accessed | tf_op | source)
XLA Modules:
  0.0 42.3 jit_solution(1551548811112099327)
XLA Ops:
  1.3 40.1 %tile_attention.1 = bf16[4,384,256]{2,1,0:T(8,128)(2,1)S(1)} custom-call(s32[1]{0:T(128)S(6)} %copy.9.clip_ref, bf16[384,256]{1,0:T(8,128)(2,1)} %bitcast.12, bf16[384,256]{1,0:T(8,128)(2,1)} %bitcast.13, bf16[384,256]{1,0:T(8,128)(2,1)} %bitcast.14, bf16[384,256]{1,0:T(8,128)(2,1)} %bitcast.15), custom_call_target="tpu_custom_call" | custom-call | tf_op jit(solution)/shard_map/tile_attention/pallas_call | solution.py:436
  41.4 0.9 %slice_bitcast_fusion = (bf16[1,1,1,384,256]{4,3,2,1,0:T(8,128)(2,1)}, bf16[1,1,1,384,256]{4,3,2,1,0:T(8,128)(2,1)}, bf16[1,1,1,384,256]{4,3,2,1,0:T(8,128)(2,1)}, bf16[1,1,1,384,256]{4,3,2,1,0:T(8,128)(2,1)}) fusion(bf16[4,384,256]{2,1,0:T(8,128)(2,1)S(1)} %tile_attention.1), kind=kLoop, calls=%fused_computation | loop fusion | bytes 1572864 | tf_op jit(solution)/shard_map/reshape;squeeze | solution.py:466
